TPU v7x, 256 devices: a whole 4x4x8 slice. The times are simulated.
256 devices in a mesh: branch: 32 (over y_hi, z, core), tensor: 8 (over y_lo, x).
Axes of the slice: x: 4, y: 4 (y_hi: 2, y_lo: 2; y = y_hi * 2 + y_lo), z: 8, core: 2. Of those that a mesh axis runs over, the one named last changes fastest.
Arguments:
- queries: bfloat16 [256, 4, 8192], P('branch', None, 'tensor'), may hold values from -72 to 72, as said below
- new_keys: bfloat16 [256, 4, 1024], P('branch', None, 'tensor'), may hold values from -12 to 12
- new_values: bfloat16 [256, 4, 1024], P('branch', None, 'tensor'), may hold values from -6 to 6
- pool_keys: bfloat16 [3072, 16, 1024], P('branch', None, 'tensor'), may hold values from -12 to 12
- pool_values: bfloat16 [3072, 16, 1024], P('branch', None, 'tensor'), may hold values from -6 to 6
- out_weight: bfloat16 [8192, 4096], P('tensor'), may hold values from -0.0625 to 0.0625
- page_table: int32 [32, 1024], replicated, may hold values from 0 to 3071, as said below
- prefix_len: int32 [32], replicated, may hold values from 8192 to 16384, as said below
- parent: int32 [256], P('branch'), may hold values from 0 to 31, as said below
- finished: int32 [256, 4], P('branch'), may hold values from 0 to 1, as said below
Outputs:
- projected: float32 [256, 4, 4096], P('branch', None, 'tensor')
Inputs may be any that keep to these rules, and one draw needn't show every extreme that they name: Each row queries[c, s] is either drawn independently of the keys, or, for some pool page p and slot r and some factor f > 1, query head h equals f times key head h // 8 of pool_keys[p, r] for every h. `page_table`: no pool page appears twice in one node's path; all paths begin with the same run of pages, nodes 4 k to 4 k + 3 share the next run, and each path ends in a run of pages that no other path holds. `prefix_len`: some node has the full 1024 * 16 tokens. Every node is the parent of exactly 8 children. Once a child has finished it stays finished at later steps.
All inputs are finite; a program needn't handle non-finite values.
Results may differ from a plain program's by a relative error of at most 0.0075.
Values may be sent and summed in bfloat16 or wider, within the bound.
No kernel may reach another device: no remote copies, remote signals or barrier semaphores. Data moves between devices by JAX's collectives and lax.ppermute only.
A program may use at most 128 MiB of HBM per device.

v0:
```python
import jax
import jax.numpy as jnp
from jax import lax
from jax.sharding import PartitionSpec as P

HD = 128
PAGE = 16
POOL_DEV = 96


NEGATIVE = -1e30


def path_counts(table_rows, lengths, first, pages):
    page_ids = first + jnp.arange(pages, dtype=jnp.int32)
    matches = (table_rows[:, :, None] == page_ids[None, None, :]).astype(jnp.bfloat16)
    width = table_rows.shape[1]
    places = (
        jnp.arange(width, dtype=jnp.int32)[:, None] * PAGE
        + jnp.arange(PAGE, dtype=jnp.int32)[None, :]
    )
    inside = (places[None, :, :] < lengths[:, None, None]).astype(jnp.bfloat16)
    counts = jnp.einsum("cjp,cjs->cps", matches, inside, preferred_element_type=jnp.float32)
    return counts.reshape(table_rows.shape[0], pages * PAGE)


def attend_block(state, query, counts, key_rows, value_rows):
    top, total, summed = state
    scores = jnp.einsum(
        "cskgd,tkd->cskgt", query, key_rows, preferred_element_type=jnp.float32
    ) * HD ** (-0.5)
    weight_mask = counts[:, None, None, None, :]
    scores = jnp.where(weight_mask > 0, scores, NEGATIVE)
    new_top = jnp.maximum(top, jnp.max(scores, axis=-1))
    factor = jnp.exp(top - new_top)
    probs = weight_mask * jnp.exp(scores - new_top[..., None])
    total = total * factor + jnp.sum(probs, axis=-1)
    summed = summed * factor[..., None] + jnp.einsum(
        "cskgt,tkd->cskgd",
        probs.astype(jnp.bfloat16),
        value_rows,
        preferred_element_type=jnp.float32,
    )
    return (new_top, total, summed)


def pool_fold(state, query, table_rows, lengths, key_piece, value_piece):
    blocks = key_piece.shape[0] // POOL_DEV
    heads = key_piece.shape[2] // HD
    key_blocks = key_piece.reshape(blocks, POOL_DEV * PAGE, heads, HD)
    value_blocks = value_piece.reshape(blocks, POOL_DEV * PAGE, heads, HD)

    def one_block(carry, inputs):
        key_rows, value_rows, number = inputs
        counts = path_counts(table_rows, lengths, number * POOL_DEV, POOL_DEV)
        return (attend_block(carry, query, counts, key_rows, value_rows), None)

    state, unused = lax.scan(
        one_block, state, (key_blocks, value_blocks, jnp.arange(blocks, dtype=jnp.int32))
    )
    return state


def finish_rows(state, query, own_keys, own_values, alive):
    top, total, summed = state
    steps = query.shape[1]
    scores = jnp.einsum(
        "cskgd,cjkd->cskgj", query, own_keys, preferred_element_type=jnp.float32
    ) * HD ** (-0.5)
    order = jnp.arange(steps, dtype=jnp.int32)
    allowed = (order[None, :] <= order[:, None])[None, :, :] & (alive[:, None, :] > 0)
    allowed = allowed[:, :, None, None, :]
    scores = jnp.where(allowed, scores, NEGATIVE)
    new_top = jnp.maximum(top, jnp.max(scores, axis=-1))
    factor = jnp.exp(top - new_top)
    probs = jnp.where(allowed, jnp.exp(scores - new_top[..., None]), 0.0)
    total = total * factor + jnp.sum(probs, axis=-1)
    summed = summed * factor[..., None] + jnp.einsum(
        "cskgj,cjkd->cskgd",
        probs.astype(jnp.bfloat16),
        own_values,
        preferred_element_type=jnp.float32,
    )
    return (summed / total[..., None]).astype(jnp.bfloat16)


def body(
    queries,
    new_keys,
    new_values,
    pool_keys,
    pool_values,
    out_weight,
    page_table,
    prefix_len,
    parent,
    finished,
):
    children, steps, width = queries.shape
    heads = new_keys.shape[2] // HD
    group = width // (heads * HD)
    query = queries.reshape(children, steps, heads, group, HD)
    own_keys = new_keys.reshape(children, steps, heads, HD)
    own_values = new_values.reshape(children, steps, heads, HD)
    alive = 1 - finished
    empty = (
        jnp.full((children, steps, heads, group), NEGATIVE, jnp.float32),
        jnp.zeros((children, steps, heads, group), jnp.float32),
        jnp.zeros((children, steps, heads, group, HD), jnp.float32),
    )
    table_rows = jnp.take(page_table, parent, axis=0)
    lengths = jnp.take(prefix_len, parent, axis=0)
    state = pool_fold(
        empty,
        query,
        table_rows,
        lengths,
        lax.all_gather(pool_keys, "branch", axis=0, tiled=True),
        lax.all_gather(pool_values, "branch", axis=0, tiled=True),
    )
    attended = finish_rows(state, query, own_keys, own_values, alive)
    flat = attended.reshape(children, steps, heads * group * HD)
    terms = jnp.einsum("csh,hd->csd", flat, out_weight, preferred_element_type=jnp.float32)
    terms = terms * alive[:, :, None].astype(jnp.float32)
    return lax.psum_scatter(terms, "tensor", scatter_dimension=2, tiled=True)


def solution(mesh):
    placed = (
        P("branch", None, "tensor"),
        P("branch", None, "tensor"),
        P("branch", None, "tensor"),
        P("branch", None, "tensor"),
        P("branch", None, "tensor"),
        P("tensor", None),
        P(),
        P(),
        P("branch"),
        P("branch", None),
    )
    return jax.shard_map(
        body, mesh=mesh, in_specs=placed, out_specs=P("branch", None, "tensor"), check_vma=False
    )
```

profile of v0, /device:TPU:16, one launch (start us, length us, event | category | flops | bytes accessed | tf_op | source)
XLA Modules:
  0.0 479.4 jit_solution(5755457555622751138)
XLA Ops:
  13.1 114.7 %all-gather.3.cloned.1.call-done = bf16[3072,16,128]{2,1,0:T(8,128)(2,1)} async-done(((bf16[96,16,128]{2,1,0:T(8,128)(2,1)}), bf16[3072,16,128]{2,1,0:T(8,128)(2,1)}) %all-gather.3.cloned.1.call-update) | async-done | bytes 12582928 | tf_op jit(solution)/shard_map/all_gather | solution.py:118
  127.8 117.0 %all-gather.5.cloned.1.call-done = bf16[3072,16,128]{2,1,0:T(8,128)(2,1)} async-done(((bf16[96,16,128]{2,1,0:T(8,128)(2,1)}), bf16[3072,16,128]{2,1,0:T(8,128)(2,1)}) %all-gather.5.cloned.1.call-update) | async-done | bytes 12582928 | tf_op jit(solution)/shard_map/all_gather | solution.py:119
  244.8 180.8 %while.15 = (s32[]{:T(128)}, f32[8,4,1,8]{3,1,0,2:T(4,128)S(1)}, f32[8,4,1,8]{3,1,0,2:T(4,128)S(1)}, f32[8,4,1,8,128]{4,3,1,0,2:T(8,128)S(1)}, s32[8,1024]{1,0:T...) while((s32[]{:T(128)}, f32[8,4,1,8]{3,1,0,2:T(4,128)S(1)}, ...), condition=%wide.region_3.4_spmd.clone, body=%wide.region_0.3_spmd.clone.sunk | while | flops 231078496 | bytes 6342597 | solution.py:58
  247.0 1.5 fusion.65
  248.5 1.5 fusion.68
  252.6 1.5 fusion.65
  254.1 1.5 fusion.68
  258.3 1.5 fusion.65
  259.8 1.5 fusion.68
  263.9 1.5 fusion.65
  265.4 1.5 fusion.68
  269.6 1.5 fusion.65
  271.1 1.5 fusion.68
  275.2 1.5 fusion.65
  276.7 1.5 fusion.68
  280.9 1.5 fusion.65
  282.4 1.5 fusion.68
  286.5 1.5 fusion.65
  288.0 1.5 fusion.68
  292.2 1.5 fusion.65
  293.7 1.5 fusion.68
  297.8 1.5 fusion.65
  299.3 1.5 fusion.68
  303.5 1.5 fusion.65
  305.0 1.5 fusion.68
  309.1 1.5 fusion.65
  310.6 1.5 fusion.68
  314.8 1.5 fusion.65
  316.3 1.5 fusion.68
  320.4 1.5 fusion.65
  321.9 1.5 fusion.68
  326.1 1.5 fusion.65
  327.6 1.5 fusion.68
  331.7 1.5 fusion.65
  333.3 1.5 fusion.68
  337.4 1.5 fusion.65
  338.9 1.5 fusion.68
  343.0 1.5 fusion.65
  344.6 1.5 fusion.68
  348.7 1.5 fusion.65
  350.2 1.5 fusion.68
  354.3 1.5 fusion.65
  355.9 1.5 fusion.68
  360.0 1.5 fusion.65
  361.5 1.5 fusion.68
  365.6 1.5 fusion.65
  367.2 1.5 fusion.68
  371.3 1.5 fusion.65
  372.8 1.5 fusion.68
  376.9 1.5 fusion.65
  382.6 1.5 fusion.65
  384.1 1.5 fusion.68
  388.2 1.5 fusion.65
  393.9 1.5 fusion.65
  399.5 1.5 fusion.65
  401.1 1.5 fusion.68
  405.2 1.5 fusion.65
  410.8 1.5 fusion.65
  416.5 1.5 fusion.65
  418.0 1.5 fusion.68
  422.1 1.5 fusion.65
  426.2 5.7 %fusion.26 = f32[8,4,4096]{2,0,1:T(8,128)} fusion(bf16[1024,4096]{1,0:T(8,128)(2,1)} %param.17, f32[8,4]{0,1:T(4,128)S(1)} %subtract_convert_fusion, bf16[8,4,1024]{2,1,0:T(4,128)(2,1)S(1)} %reshape.142), kind=kOutput, calls=%fused_computation.39 | convolution fusion | flops 268566528 | bytes 8978560 | tf_op jit(solution)/shard_map/csh,hd->csd/dot_general | solution.py:123
  431.9 39.5 %reduce-scatter.2.cloned.1.call-done = f32[8,4,512]{2,0,1:T(8,128)} async-done(((f32[8,4,4096]{2,0,1:T(8,128)}), f32[8,4,512]{2,0,1:T(8,128)}) %reduce-scatter.2.cloned.1.call-update) | async-done | bytes 65552 | tf_op jit(solution)/shard_map/reduce_scatter | solution.py:125
  471.4 1.5 copy.23
  (397 shorter events, 79.3 us)
Async XLA Ops:
  6.5 5.3 %copy-start = (s32[32,1024]{1,0:T(8,128)S(1)}, s32[32,1024]{1,0:T(8,128)}, u32[]{:S(2)}) copy-start(s32[32,1024]{1,0:T(8,128)} %param.18) | copy-start | bytes 393220
  6.5 6.0 %copy-start.2 = (s32[8]{0:T(128)S(1)}, s32[8]{0:T(128)}, u32[]{:S(2)}) copy-start(s32[8]{0:T(128)} %param.20) | copy-start | bytes 100
  6.5 5.9 %copy-start.1 = (s32[8,4]{0,1:T(4,128)S(1)}, s32[8,4]{0,1:T(4,128)}, u32[]{:S(2)}) copy-start(s32[8,4]{0,1:T(4,128)} %param.21) | copy-start | bytes 388
  6.5 6.1 %copy-start.3 = (bf16[8,4,128]{2,1,0:T(4,128)(2,1)S(1)}, bf16[8,4,128]{2,1,0:T(4,128)(2,1)}, u32[]{:S(2)}) copy-start(bf16[8,4,128]{2,1,0:T(4,128)(2,1)} %param.13) | copy-start | bytes 24580
  6.5 121.2 %all-gather.3.cloned.1.call-start = ((), (), s32[]{:S(2)}) async-start(), calls=%async_computation.1 | async-start | bytes 12976128 | tf_op jit(solution)/shard_map/all_gather | solution.py:118
  7.3 237.5 %all-gather.5.cloned.1.call-start = ((), (), s32[]{:S(2)}) async-start(), calls=%async_computation.2 | async-start | bytes 12976128 | tf_op jit(solution)/shard_map/all_gather | solution.py:119
  8.0 463.3 %reduce-scatter.2.cloned.1.call-start = ((), (), s32[]{:S(2)}) async-start(), calls=%async_computation.3 | async-start | bytes 589824 | tf_op jit(solution)/shard_map/reduce_scatter | solution.py:125
  244.8 181.0 %copy-start.4 = (bf16[8,4,128]{2,1,0:T(4,128)(2,1)S(1)}, bf16[8,4,128]{2,1,0:T(4,128)(2,1)}, u32[]{:S(2)}) copy-start(bf16[8,4,128]{2,1,0:T(4,128)(2,1)} %param.14) | copy-start | bytes 24580
Sparse Core Ops, SparseCore 0:
  10.1 117.5 all-gather.2
  130.5 114.1 all-gather.4
  432.0 39.2 reduce-scatter.1
where the time goes:
time: 483 us; the launch traced here: 479 us
  waiting for transfers between devices  273 us (57%)
  matrix products  122 us (25%)
  local copies, waits for them, and re-layouts  31.7 us (7%)
  loops' own time  23.1 us (5%)
  other arithmetic  16.4 us (3%)
  between operations  13.2 us (3%)
    all_gather x1, waiting for transfers between devices, body(): lax.all_gather(pool_values, 'branch', axis=0, tiled=True)  117 us
    all_gather x1, waiting for transfers between devices, body(): lax.all_gather(pool_keys, 'branch', axis=0, tiled=True)  115 us
    dot_general x32, matrix products, attend_block(): jnp.einsum('cskgd,tkd->cskgt', query, key_rows, preferred_element_type=jn...  47.5 us
    dot_general x32, matrix products, attend_block(): jnp.einsum('cskgt,tkd->cskgd', probs.astype(jnp.bfloat16), value_rows, pr...  46.7 us
    reduce_scatter x1, waiting for transfers between devices, body(): return lax.psum_scatter(terms, 'tensor', scatter_dimension=2, tiled=True)  39.5 us
    another operation x1, loops' own time, pool_fold(): lax.scan(one_block, state, (key_blocks, value_blocks, jnp.arange(blocks,...  23.1 us
    dot_general x32, matrix products, path_counts(): jnp.einsum('cjp,cjs->cps', matches, inside, preferred_element_type=jnp.fl...  21.6 us
    dynamic_slice x32, local copies, waits for them, and re-layouts, pool_fold(): lax.scan(one_block, state, (key_blocks, value_blocks, jnp.arange(blocks,...  19.6 us
  transfers between devices with their start and end apart: 3, of which 3 were waited for; matrix products, arithmetic and copies ran while one was open for 1% of the time, Pallas kernels for 0%

commit v1 on v0

v1 whole, which is shorter than its diff:
```python
import functools

import jax
import jax.numpy as jnp
from jax import lax
from jax.experimental import pallas as pl
from jax.experimental.pallas import tpu as pltpu
from jax.sharding import Mesh, PartitionSpec as P

HD = 128
PAGE = 16
PAGES_DEV = 96
GROUPS = 4
RING = 8
ROWS = 256
HEADS = 8
CS = 32
TILE = 1024
BIG = 2.0**100
LOW = -3.0e38
C2 = HD**-0.5 * 1.4426950408889634
MIB = 1024 * 1024


def mask_kernel(first_ref, table_ref, left_ref, count_ref, bias_ref):
    left = left_ref[...]
    for block in range(GROUPS):
        first = first_ref[block]

        def one_page(page, carry, block=block, first=first):
            hit = jnp.where(table_ref[...] == first + page, left, 0)
            count_ref[pl.ds(block * PAGES_DEV + page, 1), :] = jnp.sum(hit, axis=0, keepdims=True)
            return carry

        lax.fori_loop(0, PAGES_DEV, one_page, 0, unroll=8)
    part = count_ref[...]
    part = part + pltpu.roll(part, 64, 1)
    count_ref[...] = part + pltpu.roll(part, 32, 1)
    token = lax.broadcasted_iota(jnp.int32, (PAGE, HD), 0)

    def one_bias(page, carry):
        held = jnp.broadcast_to(count_ref[pl.ds(page, 1), :], (PAGE, HD))
        bias = jnp.where(token >= held, -BIG, 0.0).astype(jnp.bfloat16)
        bias_ref[pl.ds(pl.multiple_of(page * PAGE, PAGE), PAGE), :] = bias
        return carry

    lax.fori_loop(0, GROUPS * PAGES_DEV, one_bias, 0, unroll=8)


def path_masks(first, table, left):
    return pl.pallas_call(
        mask_kernel,
        out_shape=(
            jax.ShapeDtypeStruct((GROUPS * PAGES_DEV, HD), jnp.int32),
            jax.ShapeDtypeStruct((GROUPS * PAGES_DEV * PAGE, HD), jnp.bfloat16),
        ),
        in_specs=[
            pl.BlockSpec(memory_space=pltpu.SMEM),
            pl.BlockSpec(memory_space=pltpu.VMEM),
            pl.BlockSpec(memory_space=pltpu.VMEM),
        ],
        out_specs=(pl.BlockSpec(memory_space=pltpu.VMEM), pl.BlockSpec(memory_space=pltpu.VMEM)),
        cost_estimate=pl.CostEstimate(flops=2**26, bytes_accessed=2**21, transcendentals=0),
        compiler_params=pltpu.CompilerParams(vmem_limit_bytes=16 * MIB),
        name="path_masks",
    )(first, table, left)


def attend_kernel(
    place_ref, tiles_ref, query_ref, a_ref, b_ref, c_ref, d_ref, bias_ref, out_ref,
    keys, values, rows, summed, top,
):
    for group, kv_ref in enumerate((a_ref, b_ref, c_ref, d_ref)):

        def one_page(page, carry, group=group, kv_ref=kv_ref):
            source = pl.ds(pl.multiple_of(page * PAGE, PAGE), PAGE)
            number = group * PAGES_DEV + page
            target = pl.ds(pl.multiple_of(place_ref[number] * PAGE, PAGE), PAGE)
            keys[target, 0:HD] = kv_ref[0, source, :]
            keys[target, HD : 2 * HD] = bias_ref[pl.ds(pl.multiple_of(number * PAGE, PAGE), PAGE), :]
            values[target, 0:HD] = kv_ref[1, source, :]
            return carry

        lax.fori_loop(0, PAGES_DEV, one_page, 0, unroll=8)
    values[:, HD : 2 * HD] = jnp.ones((values.shape[0], HD), jnp.bfloat16)
    for block in range(RING):
        held = query_ref[block]
        for head in range(HEADS):
            at = block * ROWS + head * CS
            rows[at : at + CS, 0:HD] = held[:, head * HD : (head + 1) * HD]
            rows[at : at + CS, HD : 2 * HD] = held[:, HEADS * HD : (HEADS + 1) * HD]
    summed[...] = jnp.zeros_like(summed)
    top[...] = jnp.full_like(top, LOW)

    def one_tile(tile, carry):
        here = pl.ds(pl.multiple_of(tile * TILE, TILE), TILE)
        for block in range(RING):
            span = slice(block * ROWS, (block + 1) * ROWS)
            scores = lax.dot_general(
                rows[span, :], keys[here, :], (((1,), (1,)), ((), ())),
                preferred_element_type=jnp.float32,
            )
            old = top[span, :]
            new = jnp.maximum(old, jnp.max(scores, axis=1, keepdims=True) * C2)
            weights = jnp.exp2(scores * C2 - new[:, 0:1]).astype(jnp.bfloat16)
            factor = jnp.exp2(old - new)
            part = jnp.dot(weights, values[here, :], preferred_element_type=jnp.float32)
            summed[span, 0:HD] = summed[span, 0:HD] * factor + part[:, 0:HD]
            summed[span, HD : 2 * HD] = summed[span, HD : 2 * HD] * factor + part[:, HD : 2 * HD]
            top[span, :] = new
        return carry

    lax.fori_loop(0, tiles_ref[0], one_tile, 0)
    diagonal = lax.broadcasted_iota(jnp.int32, (HD, HD), 0) == lax.broadcasted_iota(jnp.int32, (HD, HD), 1)
    for block in range(RING):
        span = slice(block * ROWS, (block + 1) * ROWS)
        total = summed[span, HD : 2 * HD]
        out_ref[block, 0:ROWS, :] = (summed[span, 0:HD] / total).astype(jnp.bfloat16)
        level = top[span, :] + jnp.log2(total)
        lines = [
            jnp.sum(jnp.where(diagonal, level[half * HD : (half + 1) * HD], 0.0), axis=0, keepdims=True)
            for half in range(2)
        ]
        line = jnp.concatenate(lines, axis=0)
        high = line.astype(jnp.bfloat16).astype(jnp.float32)
        middle = (line - high).astype(jnp.bfloat16).astype(jnp.float32)
        low = line - high - middle
        tail = jnp.concatenate([high, middle, low, jnp.zeros((10, HD), jnp.float32)], axis=0)
        out_ref[block, ROWS : ROWS + 16, :] = tail.astype(jnp.bfloat16)


def attend(place, tiles, query, kvs, bias):
    tokens = GROUPS * PAGES_DEV * PAGE
    vmem = pl.BlockSpec(memory_space=pltpu.VMEM)
    smem = pl.BlockSpec(memory_space=pltpu.SMEM)
    return pl.pallas_call(
        attend_kernel,
        out_shape=jax.ShapeDtypeStruct((RING, ROWS + 16, HD), jnp.bfloat16),
        in_specs=[smem, smem] + [vmem] * 6,
        out_specs=vmem,
        scratch_shapes=[
            pltpu.VMEM((tokens, 2 * HD), jnp.bfloat16),
            pltpu.VMEM((tokens, 2 * HD), jnp.bfloat16),
            pltpu.VMEM((RING * ROWS, 2 * HD), jnp.bfloat16),
            pltpu.VMEM((RING * ROWS, 2 * HD), jnp.float32),
            pltpu.VMEM((RING * ROWS, HD), jnp.float32),
        ],
        cost_estimate=pl.CostEstimate(flops=2**33, bytes_accessed=2**23, transcendentals=2**23),
        compiler_params=pltpu.CompilerParams(vmem_limit_bytes=48 * MIB),
        name="attend",
    )(place, tiles, query, *kvs, bias)


def finish_kernel(
    parts_ref, query_ref, key_ref, value_ref, allowed_ref, alive_ref, weight_ref, out_ref, attended
):
    @pl.when(pl.program_id(0) == 0)
    def merge():
        diagonal = lax.broadcasted_iota(jnp.int32, (HD, HD), 0) == lax.broadcasted_iota(jnp.int32, (HD, HD), 1)
        levels = []
        for block in range(RING):
            tail = parts_ref[block, ROWS : ROWS + 16, :].astype(jnp.float32)
            line = tail[0:2] + tail[2:4] + tail[4:6]
            columns = [
                jnp.sum(jnp.where(diagonal, jnp.broadcast_to(line[half : half + 1], (HD, HD)), 0.0), axis=1, keepdims=True)
                for half in range(2)
            ]
            levels.append(jnp.concatenate(columns, axis=0))
        query = jnp.concatenate([query_ref[:, head * HD : (head + 1) * HD] for head in range(HEADS)], axis=0)
        scores = lax.dot_general(
            query, key_ref[...], (((1,), (1,)), ((), ())), preferred_element_type=jnp.float32
        )
        allowed = jnp.concatenate([allowed_ref[...]] * HEADS, axis=0) > 0
        scores = jnp.where(allowed, scores * C2, -BIG)
        own_top = jnp.max(scores, axis=1, keepdims=True)
        own = jnp.where(allowed, jnp.exp2(scores - own_top), 0.0)
        own_sum = jnp.dot(own.astype(jnp.bfloat16), value_ref[...], preferred_element_type=jnp.float32)
        best = own_top
        for level in levels:
            best = jnp.maximum(best, level)
        factor = jnp.exp2(own_top - best)
        total = factor * jnp.sum(own, axis=1, keepdims=True)
        summed = factor * own_sum
        for block in range(RING):
            factor = jnp.exp2(levels[block] - best)
            total = total + factor
            summed = summed + factor * parts_ref[block, 0:ROWS, :].astype(jnp.float32)
        result = (summed / total).astype(jnp.bfloat16)
        for head in range(HEADS):
            attended[:, head * HD : (head + 1) * HD] = result[head * CS : (head + 1) * CS, :]

    terms = jnp.dot(attended[...], weight_ref[...], preferred_element_type=jnp.float32)
    out_ref[0] = (terms * alive_ref[...]).astype(jnp.bfloat16)


def finish(parts, query, keys, values, allowed, alive, weight):
    blocks = 8
    width = weight.shape[1] // blocks

    def whole(shape):
        return pl.BlockSpec(shape, lambda i: (0,) * len(shape))

    return pl.pallas_call(
        finish_kernel,
        grid=(blocks,),
        out_shape=jax.ShapeDtypeStruct((blocks, CS, width), jnp.bfloat16),
        in_specs=[
            whole(parts.shape),
            whole(query.shape),
            whole(keys.shape),
            whole(values.shape),
            whole(allowed.shape),
            whole(alive.shape),
            pl.BlockSpec((weight.shape[0], width), lambda i: (0, i)),
        ],
        out_specs=pl.BlockSpec((1, CS, width), lambda i: (i, 0, 0)),
        scratch_shapes=[pltpu.VMEM((CS, HEADS * HD), jnp.bfloat16)],
        cost_estimate=pl.CostEstimate(flops=2**28, bytes_accessed=2**23, transcendentals=0),
        compiler_params=pltpu.CompilerParams(vmem_limit_bytes=32 * MIB),
        name="finish",
    )(parts, query, keys, values, allowed, alive, weight)


def body(
    queries, new_keys, new_values, pool_keys, pool_values, out_weight, page_table, prefix_len, parent, finished
):
    children, steps, width = queries.shape
    rows = children * steps
    nodes, path_pages = page_table.shape
    query = queries.reshape(rows, width)
    node_of_row = jnp.repeat(parent, steps)
    hot = (node_of_row[:, None] == jnp.arange(HD, dtype=jnp.int32)[None, :]).astype(jnp.bfloat16)
    sent = jnp.concatenate([query, hot], axis=1)
    gathered = lax.all_to_all(
        jnp.broadcast_to(sent[None], (RING,) + sent.shape), "z", split_axis=0, concat_axis=0, tiled=True
    )

    swap = [(0, 1), (1, 0)]
    kv = jnp.stack([pool_keys.reshape(PAGES_DEV * PAGE, HD), pool_values.reshape(PAGES_DEV * PAGE, HD)])
    kv_far = lax.ppermute(kv, "yh", swap)
    kv_core = lax.ppermute(kv, "c", swap)
    kv_far_core = lax.ppermute(kv_far, "c", swap)
    yh, z, core = lax.axis_index("yh"), lax.axis_index("z"), lax.axis_index("c")
    first = jnp.stack(
        [
            PAGES_DEV * ((a * RING + z) * 2 + b)
            for a, b in ((yh, core), (yh, 1 - core), (1 - yh, core), (1 - yh, 1 - core))
        ]
    ).astype(jnp.int32)
    table = page_table.T.reshape(nodes * path_pages // HD, HD)
    place = jnp.arange(path_pages, dtype=jnp.int32)
    left = jnp.clip(prefix_len[None, :] - PAGE * place[:, None], 0, PAGE).reshape(table.shape)
    count, bias = path_masks(first, table, left)
    uses = jnp.sum((count[:, :nodes] > 0).astype(jnp.int32), axis=1)
    order = jnp.arange(uses.shape[0], dtype=jnp.int32)
    before = (uses[None, :] > uses[:, None]) | ((uses[None, :] == uses[:, None]) & (order[None, :] < order[:, None]))
    rank = jnp.sum(before.astype(jnp.int32), axis=1)
    used = jnp.sum((uses > 0).astype(jnp.int32))
    tiles = jnp.maximum((used * PAGE + TILE - 1) // TILE, 1).reshape(1)
    parts = attend(rank, tiles, gathered, (kv, kv_core, kv_far, kv_far_core), bias)
    parts = lax.all_to_all(parts, "z", split_axis=0, concat_axis=0, tiled=True)

    alive = 1 - finished
    child = jnp.arange(rows, dtype=jnp.int32) // steps
    step = jnp.arange(rows, dtype=jnp.int32) % steps
    allowed = (
        (child[:, None] == child[None, :])
        & (step[None, :] <= step[:, None])
        & (alive.reshape(1, rows) > 0)
    ).astype(jnp.int32)
    terms = finish(
        parts,
        query,
        new_keys.reshape(rows, HD),
        new_values.reshape(rows, HD),
        allowed,
        alive.reshape(rows, 1).astype(jnp.float32),
        out_weight,
    )
    terms = lax.all_to_all(terms, ("yl", "x"), split_axis=0, concat_axis=0, tiled=True)
    return jnp.sum(terms.astype(jnp.float32), axis=0).reshape(children, steps, terms.shape[-1])


def solution(mesh):
    fine = Mesh(mesh.devices.reshape(2, RING, 2, 2, 4), ("yh", "z", "c", "yl", "x"))
    branch, tensor = ("yh", "z", "c"), ("yl", "x")
    placed = (
        P(branch, None, tensor),
        P(branch, None, tensor),
        P(branch, None, tensor),
        P(branch, None, tensor),
        P(branch, None, tensor),
        P(tensor, None),
        P(),
        P(),
        P(branch),
        P(branch, None),
    )
    return jax.shard_map(
        body, mesh=fine, in_specs=placed, out_specs=P(branch, None, tensor), check_vma=False
    )
```

time: 483 us -> 95.6 us (0.20)
  waiting for transfers between devices: 273 us -> 26.6 us
  matrix products: 122 us -> 0 us
  loops' own time: 23.1 us -> 0 us
  Pallas kernels: 0 us -> 23 us
  local copies, waits for them, and re-layouts: 31.7 us -> 9.03 us
  starting transfers between devices: 0.11 us -> 20.8 us
  other arithmetic: 16.4 us -> 2.53 us
  between operations: 13.2 us -> 0.81 us
  blocking collectives: 0 us -> 12.3 us
    all_gather x2 -> x0, waiting for transfers between devices: 232 us -> none  [the longest x1 117 us: body(): lax.all_gather(pool_values, 'branch', axis=0, tiled=True)]
    dot_general x99 -> x0, matrix products: 122 us -> none  [the longest x32 47.5 us: attend_block(): jnp.einsum('cskgd,tkd->cskgt', query, key_rows, preferred_element_type=jn...]
    reduce_scatter x1 -> x0, waiting for transfers between devices: 39.5 us -> none  [body(): return lax.psum_scatter(terms, 'tensor', scatter_dimension=2, tiled=True)]
    another operation x1 -> x0, loops' own time: 23.1 us -> none  [pool_fold(): lax.scan(one_block, state, (key_blocks, value_blocks, jnp.arange(blocks,...]
    pallas_call x0 -> x3, Pallas kernels: none -> 23 us  [the longest x1 11.9 us: attend(): pl.pallas_call(attend_kernel, out_shape=jax.ShapeDtypeStruct((RING, ROWS...]
    dynamic_slice x32 -> x0, local copies, waits for them, and re-layouts: 19.6 us -> none  [pool_fold(): lax.scan(one_block, state, (key_blocks, value_blocks, jnp.arange(blocks,...]
    all_to_all x0 -> x2, starting transfers between devices: none -> 18.6 us  [the longest x1 11.9 us: body(): parts = lax.all_to_all(parts, 'z', split_axis=0, concat_axis=0, tiled=True)]
    all_to_all x0 -> x2, waiting for transfers between devices: none -> 18.5 us  [the longest x1 18.5 us: body(): parts = lax.all_to_all(parts, 'z', split_axis=0, concat_axis=0, tiled=True)]
  transfers between devices with their start and end apart: 3 -> 5, of which waited for: 3 -> 2; matrix products, arithmetic and copies ran while one was open for 1% -> 7% of each run, Pallas kernels for 0% -> 8%
where the time goes in v1:
time: 95.6 us; the launch traced here: 95.1 us
  waiting for transfers between devices  26.6 us (28%)
  Pallas kernels  23 us (24%)
  starting transfers between devices  20.8 us (22%)
  blocking collectives  12.3 us (13%)
  local copies, waits for them, and re-layouts  9.03 us (9%)
  other arithmetic  2.53 us (3%)
    all_to_all x1, waiting for transfers between devices, body(): parts = lax.all_to_all(parts, 'z', split_axis=0, concat_axis=0, tiled=True)  18.5 us
    all_to_all x1, blocking collectives, body(): lax.all_to_all(terms, ('yl', 'x'), split_axis=0, concat_axis=0, tiled=True)  12.3 us
    pallas_call x1, Pallas kernels, attend(): pl.pallas_call(attend_kernel, out_shape=jax.ShapeDtypeStruct((RING, ROWS...  11.9 us
    all_to_all x1, starting transfers between devices, body(): parts = lax.all_to_all(parts, 'z', split_axis=0, concat_axis=0, tiled=True)  11.9 us
    ppermute x1, waiting for transfers between devices, body(): kv_far = lax.ppermute(kv, 'yh', swap)  8.17 us
    pallas_call x1, Pallas kernels, path_masks(): pl.pallas_call(mask_kernel, out_shape=(jax.ShapeDtypeStruct((GROUPS * PAG...  7.25 us
    all_to_all x1, starting transfers between devices, body(): lax.all_to_all(jnp.broadcast_to(sent[None], (RING,) + sent.shape), 'z', s...  6.73 us
    pallas_call x1, Pallas kernels, finish(): pl.pallas_call(finish_kernel, grid=(blocks,), out_shape=jax.ShapeDtypeStr...  3.85 us
  transfers between devices with their start and end apart: 5, of which 2 were waited for; matrix products, arithmetic and copies ran while one was open for 7% of the time, Pallas kernels for 8%

profile of v1, /device:TPU:16, one launch (start us, length us, event | category | flops | bytes accessed | tf_op | source)
XLA Modules:
  0.0 95.1 jit_solution(589368400416807956)
XLA Ops:
  0.0 1.2 %pad_maximum_fusion.a_ref = bf16[2,1536,128]{2,1,0:T(8,128)(2,1)S(1)} fusion(bf16[1,1536,128]{2,1,0:T(8,128)(2,1)} %bitcast.14, bf16[1,1536,128]{2,1,0:T(8,128)(2,1)} %bitcast.15), kind=kLoop, calls=%fused_computation | loop fusion | flops 393216 | bytes 1572864 | tf_op jit(solution)/shard_map/stack | solution.py:239
  1.2 2.2 %collective-permute-start.1 = (bf16[2,1536,128]{2,1,0:T(8,128)(2,1)S(1)}, bf16[2,1536,128]{2,1,0:T(8,128)(2,1)}, u32[]{:S(2)}, u32[]{:S(2)}) collective-permute-start(bf16[2,1536,128]{2,1,0:T(8,128)(2,1)S(1)} %pad_maximum_fusion.a_ref), channel_id=1, source_target_pairs={{0,128},{128,0},{1,129},{129,1},{2,130},{130,2},{3,131},{131,3},{4... | collective-permute-start | bytes 2359304 | tf_op jit(solution)/shard_map/ppermute | solution.py:240
  3.3 0.7 broadcast_in_dim.4
  4.1 0.1 eq.19
  4.2 0.9 reshape.103.query_ref
  5.0 0.1 fusion.2
  5.1 0.9 broadcast_in_dim.5
  6.0 6.7 %all-to-all-start = ((bf16[8,32,1152]{2,1,0:T(8,128)(2,1)}), bf16[8,32,1152]{2,1,0:T(8,128)(2,1)S(1)}, u32[]{:S(2)}, u32[]{:S(2)}) async-start(bf16[8,32,1152]{2,1,0:T(8,128)(2,1)} %broadcast_in_dim.5), calls=%async_computation | async-start | bytes 1179648 | tf_op jit(solution)/shard_map/all_to_all | solution.py:234
  12.7 0.0 collective-permute-start
  12.7 1.1 %copy.20 = s32[1024,32]{1,0:T(8,128)S(1)} copy(s32[1024,32]{0,1:T(8,128)} %bitcast.16) | data formatting | bytes 262144 | tf_op jit(solution)/shard_map/transpose | solution.py:250
  13.8 0.2 reshape.101.table_ref
  14.0 8.2 %collective-permute-done.1.c_ref = bf16[2,1536,128]{2,1,0:T(8,128)(2,1)} collective-permute-done((bf16[2,1536,128]{2,1,0:T(8,128)(2,1)S(1)}, bf16[2,1536,128]{2,1,0:T(8,128)(2,1)}, u32[]{:S(2)}, u32[]{:S(2)}) %collective-permute-start.1) | collective-permute-done | bytes 786464 | tf_op jit(solution)/shard_map/ppermute | solution.py:240
  22.2 0.0 collective-permute-start.2
  22.2 0.1 copy.21
  22.3 0.7 sub.49
  23.0 0.1 sub.50
  23.0 0.1 pad_add_fusion.first_ref
  23.1 7.2 %path_masks.1 = (s32[384,128]{1,0:T(8,128)S(1)}, bf16[6144,128]{1,0:T(8,128)(2,1)S(1)}) custom-call(s32[4]{0:T(128)S(1)} %pad_add_fusion.first_ref, s32[256,128]{1,0:T(8,128)S(1)} %reshape.101.table_ref, s32[256,128]{1,0:T(8,128)S(1)} %subtract_clamp_fusion.left_ref), custom_call_target="tpu_custom_call" | custom-call | flops 67108864 | bytes 2097152 | tf_op jit(solution)/shard_map/path_masks/pallas_call | solution.py:51
  30.4 0.1 convert_reduce_fusion.2
  30.5 0.6 convert_reduce_fusion.3
  31.9 0.2 convert_reduce_fusion.place_ref
  32.1 0.0 collective-permute-done.b_ref
  32.1 0.0 all-to-all-done.query_ref
  32.1 0.0 collective-permute-done.2.d_ref
  32.1 0.0 copy-start.3
  32.1 0.0 copy-start.1
  32.2 0.0 copy-start.2
  32.2 11.9 %attend.1 = bf16[8,272,128]{2,1,0:T(8,128)(2,1)} custom-call(s32[384]{0:T(512)S(1)} %convert_reduce_fusion.place_ref, s32[1]{0:T(128)} %bitcast.6.tiles_ref, bf16[8,32,1152]{2,1,0:T(8,128)(2,1)S(1)} %all-to-all-done.query_ref, bf16[2,1536,128]{2,1,0:T(8,128)(2,1)S(1)} %pad_maximum_fusion.a_ref, bf16[2,1536,128]{2,1,0:T(8,128)(2,1)} %collective-permute-done.b_ref, ...), custom_call_target="tpu_custom_call" | custom-call | flops 8589934592 | bytes 8388608 | tf_op jit(solution)/shard_map/attend/pallas_call | solution.py:136
  44.1 11.9 %all-to-all-start.1 = ((bf16[8,272,128]{2,1,0:T(8,128)(2,1)}), bf16[8,272,128]{2,1,0:T(8,128)(2,1)S(1)}, u32[]{:S(2)}, u32[]{:S(2)}) async-start(bf16[8,272,128]{2,1,0:T(8,128)(2,1)} %attend.1), calls=%async_computation.1 | async-start | bytes 1114112 | tf_op jit(solution)/shard_map/all_to_all | solution.py:261
  56.0 0.0 copy-done.3
  56.0 0.1 copy.22
  56.1 0.1 gt.45
  56.2 0.1 copy.23
  56.2 0.1 convert_element_type.31.alive_ref
  56.3 0.1 and_convert_fusion.allowed_ref
  56.4 18.5 %all-to-all-done.1.parts_ref = bf16[8,272,128]{2,1,0:T(8,128)(2,1)S(1)} async-done(((bf16[8,272,128]{2,1,0:T(8,128)(2,1)}), bf16[8,272,128]{2,1,0:T(8,128)(2,1)S(1)}, u32[]{:S(2)}, u32[]{:S(2)}) %all-to-all-start.1) | async-done | bytes 557088 | tf_op jit(solution)/shard_map/all_to_all | solution.py:261
  74.9 0.0 copy-done.1
  74.9 0.0 copy-done.2
  74.9 0.0 copy-start
  74.9 3.4 %copy-done = bf16[1024,4096]{1,0:T(8,128)(2,1)S(1)} copy-done((bf16[1024,4096]{1,0:T(8,128)(2,1)S(1)}, bf16[1024,4096]{1,0:T(8,128)(2,1)}, u32[]{:S(2)}) %copy-start) | copy-done | bytes 8388632
  78.3 3.9 %finish.1 = bf16[8,32,512]{2,1,0:T(8,128)(2,1)S(1)} custom-call(bf16[8,272,128]{2,1,0:T(8,128)(2,1)S(1)} %all-to-all-done.1.parts_ref, bf16[32,1024]{1,0:T(8,128)(2,1)S(1)} %reshape.103.query_ref, bf16[32,128]{1,0:T(8,128)(2,1)S(1)} %bitcast.11, bf16[32,128]{1,0:T(8,128)(2,1)S(1)} %bitcast.12, s32[32,32]{1,0:T(8,128)S(1)} %and_convert_fusion.allowed_ref, ...), custom_call_target="tpu_custom_call" | custom-call | flops 268435456 | bytes 8388608 | tf_op jit(solution)/shard_map/finish/pallas_call | solution.py:203
  82.1 12.3 %all_to_all.15 = bf16[8,32,512]{2,1,0:T(8,128)(2,1)S(1)} all-to-all(bf16[8,32,512]{2,1,0:T(8,128)(2,1)S(1)} %finish.1), channel_id=1, replica_groups=mesh['yh'=2,'z'=8,'c'=2,'yl'=2,'x'=4] {'yl','x'}, dimensions={0} | all-to-all | bytes 524288 | tf_op jit(solution)/shard_map/all_to_all | solution.py:280
  94.4 0.7 reshape.106
  (8 shorter events, 0.1 us)
Async XLA Ops:
  1.2 21.0 %collective-permute-start.1 = (bf16[2,1536,128]{2,1,0:T(8,128)(2,1)S(1)}, bf16[2,1536,128]{2,1,0:T(8,128)(2,1)}, u32[]{:S(2)}, u32[]{:S(2)}) collective-permute-start(bf16[2,1536,128]{2,1,0:T(8,128)(2,1)S(1)} %pad_maximum_fusion.a_ref), channel_id=1, source_target_pairs={{0,128},{128,0},{1,129},{129,1},{2,130},{130,2},{3,131},{131,3},{4... | collective-permute-start | bytes 2359304 | tf_op jit(solution)/shard_map/ppermute | solution.py:240
  6.0 26.2 %all-to-all-start = ((bf16[8,32,1152]{2,1,0:T(8,128)(2,1)}), bf16[8,32,1152]{2,1,0:T(8,128)(2,1)S(1)}, u32[]{:S(2)}, u32[]{:S(2)}) async-start(bf16[8,32,1152]{2,1,0:T(8,128)(2,1)} %broadcast_in_dim.5), calls=%async_computation | async-start | bytes 1179648 | tf_op jit(solution)/shard_map/all_to_all | solution.py:234
  12.7 19.4 %collective-permute-start = (bf16[2,1536,128]{2,1,0:T(8,128)(2,1)S(1)}, bf16[2,1536,128]{2,1,0:T(8,128)(2,1)}, u32[]{:S(2)}, u32[]{:S(2)}) collective-permute-start(bf16[2,1536,128]{2,1,0:T(8,128)(2,1)S(1)} %pad_maximum_fusion.a_ref), channel_id=1, source_target_pairs={{0,8},{8,0},{1,9},{9,1},{2,10},{10,2},{3,11},{11,3},{4,12},{12,4},... | collective-permute-start | bytes 2359304 | tf_op jit(solution)/shard_map/ppermute | solution.py:241
  22.2 10.0 %collective-permute-start.2 = (bf16[2,1536,128]{2,1,0:T(8,128)(2,1)}, bf16[2,1536,128]{2,1,0:T(8,128)(2,1)}, u32[]{:S(2)}, u32[]{:S(2)}) collective-permute-start(bf16[2,1536,128]{2,1,0:T(8,128)(2,1)} %collective-permute-done.1.c_ref), channel_id=1, source_target_pairs={{0,8},{8,0},{1,9},{9,1},{2,10},{10,2},{3,11},{11,3},{4,12},{12,4},... | collective-permute-start | bytes 2359304 | tf_op jit(solution)/shard_map/ppermute | solution.py:242
  32.1 23.8 %copy-start.3 = (s32[8,4]{0,1:T(4,128)S(1)}, s32[8,4]{0,1:T(4,128)}, u32[]{:S(2)}) copy-start(s32[8,4]{0,1:T(4,128)} %param.19) | copy-start | bytes 388
  32.1 42.7 %copy-start.1 = (bf16[8,4,128]{2,1,0:T(4,128)(2,1)S(1)}, bf16[8,4,128]{2,1,0:T(4,128)(2,1)}, u32[]{:S(2)}) copy-start(bf16[8,4,128]{2,1,0:T(4,128)(2,1)} %param.11) | copy-start | bytes 24580
  32.2 42.7 %copy-start.2 = (bf16[8,4,128]{2,1,0:T(4,128)(2,1)S(1)}, bf16[8,4,128]{2,1,0:T(4,128)(2,1)}, u32[]{:S(2)}) copy-start(bf16[8,4,128]{2,1,0:T(4,128)(2,1)} %param.12) | copy-start | bytes 24580
  44.1 30.8 %all-to-all-start.1 = ((bf16[8,272,128]{2,1,0:T(8,128)(2,1)}), bf16[8,272,128]{2,1,0:T(8,128)(2,1)S(1)}, u32[]{:S(2)}, u32[]{:S(2)}) async-start(bf16[8,272,128]{2,1,0:T(8,128)(2,1)} %attend.1), calls=%async_computation.1 | async-start | bytes 1114112 | tf_op jit(solution)/shard_map/all_to_all | solution.py:261
  74.9 3.4 %copy-start = (bf16[1024,4096]{1,0:T(8,128)(2,1)S(1)}, bf16[1024,4096]{1,0:T(8,128)(2,1)}, u32[]{:S(2)}) copy-start(bf16[1024,4096]{1,0:T(8,128)(2,1)} %weight_ref.1) | copy-start | bytes 25165828

commit v2 on v1

v2 whole, which is shorter than its diff:
```python
import functools

import jax
import jax.numpy as jnp
from jax import lax
from jax.experimental import pallas as pl
from jax.experimental.pallas import tpu as pltpu
from jax.sharding import Mesh, PartitionSpec as P

HD = 128
PAGE = 16
PAGES_DEV = 96
GROUPS = 4
RING = 8
ROWS = 256
HEADS = 8
CS = 32
UNROLL = 8
TOGETHER = 2
SIZES = (2304, 2560, 6144)
BIG = 2.0**100
C2 = HD**-0.5 * 1.4426950408889634
MIB = 1024 * 1024


def cost(microseconds):
    return pl.CostEstimate(flops=int(microseconds * 1.15e9), bytes_accessed=2**16, transcendentals=0)


def prepare_kernel(parent_ref, query_ref, out_ref, wide):
    lane = lax.broadcasted_iota(jnp.int32, (4, HD), 1)
    for child in range(8):
        rows = slice(child * 4, child * 4 + 4)
        wide[rows, 0 : HEADS * HD] = query_ref[child].astype(jnp.float32)
        wide[rows, HEADS * HD : (HEADS + 1) * HD] = jnp.where(lane == parent_ref[child], 1.0, 0.0)
    held = wide[...].astype(jnp.bfloat16)
    for copy in range(RING):
        out_ref[copy] = held


def prepare(parent, queries):
    return pl.pallas_call(
        prepare_kernel,
        out_shape=jax.ShapeDtypeStruct((RING, CS, (HEADS + 1) * HD), jnp.bfloat16),
        in_specs=[pl.BlockSpec(memory_space=pltpu.SMEM), pl.BlockSpec(memory_space=pltpu.VMEM)],
        out_specs=pl.BlockSpec(memory_space=pltpu.VMEM),
        scratch_shapes=[pltpu.VMEM((CS, (HEADS + 1) * HD), jnp.float32)],
        cost_estimate=cost(1.0),
        compiler_params=pltpu.CompilerParams(vmem_limit_bytes=60 * MIB),
        name="prepare",
    )(parent, queries)


def mask_kernel(first_ref, table_ref, left_ref, count_ref):
    left = left_ref[...]
    for block in range(GROUPS):
        first = first_ref[block]

        def one_page(page, carry, block=block, first=first):
            hit = jnp.where(table_ref[...] == first + page, left, 0)
            count_ref[pl.ds(block * PAGES_DEV + page, 1), :] = jnp.sum(hit, axis=0, keepdims=True)
            return carry

        lax.fori_loop(0, PAGES_DEV, one_page, 0, unroll=8)
    part = count_ref[...]
    part = part + pltpu.roll(part, 64, 1)
    count_ref[...] = part + pltpu.roll(part, 32, 1)


def path_masks(first, table, left):
    return pl.pallas_call(
        mask_kernel,
        out_shape=jax.ShapeDtypeStruct((GROUPS * PAGES_DEV, HD), jnp.int32),
        in_specs=[
            pl.BlockSpec(memory_space=pltpu.SMEM),
            pl.BlockSpec(memory_space=pltpu.VMEM),
            pl.BlockSpec(memory_space=pltpu.VMEM),
        ],
        out_specs=pl.BlockSpec(memory_space=pltpu.VMEM),
        cost_estimate=cost(7.0),
        compiler_params=pltpu.CompilerParams(vmem_limit_bytes=16 * MIB),
        name="path_masks",
    )(first, table, left)


def attend_tokens(tokens, rows, keys, values, levels, out_ref):
    def span(block):
        return pl.ds(pl.multiple_of(block * ROWS, ROWS), ROWS)

    def score(block):
        return lax.dot_general(
            rows[span(block), :], keys[0:tokens, :], (((1,), (1,)), ((), ())),
            preferred_element_type=jnp.float32,
        )

    def weigh(scores):
        top = jnp.max(scores, axis=1, keepdims=True) * C2
        return top, jnp.exp2(scores * C2 - top).astype(jnp.bfloat16)

    def store(block, top, weights):
        summed = jnp.dot(weights, values[0:tokens, :], preferred_element_type=jnp.float32)
        total = summed[:, HD : 2 * HD]
        out_ref[block, 0:ROWS, :] = (summed[:, 0:HD] / total).astype(jnp.bfloat16)
        levels[span(block), :] = top + jnp.log2(total)

    def some_blocks(step, carry):
        first = step * TOGETHER
        scores, held = score(first), None
        for index in range(TOGETHER):
            following = score(first + index + 1) if index + 1 < TOGETHER else None
            top, weights = weigh(scores)
            if held is not None:
                store(*held)
            held, scores = (first + index, top, weights), following
        store(*held)
        return carry

    lax.fori_loop(0, RING // TOGETHER, some_blocks, 0)


def attend_kernel(
    list_ref, used_ref, query_ref, ka_ref, va_ref, kb_ref, vb_ref, kc_ref, vc_ref, kd_ref, vd_ref,
    count_ref, out_ref, keys, values, rows, levels,
):
    token = lax.broadcasted_iota(jnp.int32, (PAGE, HD), 0)
    pool = ((ka_ref, va_ref), (kb_ref, vb_ref), (kc_ref, vc_ref), (kd_ref, vd_ref))
    filled = jnp.int32(0)
    for group, (key_ref, value_ref) in enumerate(pool):

        def some_pages(step, carry, group=group, key_ref=key_ref, value_ref=value_ref, filled=filled):
            for lane in range(UNROLL):
                page = list_ref[group * PAGES_DEV + step * UNROLL + lane]
                target = pl.ds(pl.multiple_of((filled + step * UNROLL + lane) * PAGE, PAGE), PAGE)
                keys[target, 0:HD] = key_ref[page]
                held = jnp.broadcast_to(count_ref[pl.ds(group * PAGES_DEV + page, 1), :], (PAGE, HD))
                keys[target, HD : 2 * HD] = jnp.where(token >= held, -BIG, 0.0).astype(jnp.bfloat16)
                values[target, 0:HD] = value_ref[page]
            return carry

        lax.fori_loop(0, (used_ref[group] + UNROLL - 1) // UNROLL, some_pages, 0)
        filled = filled + used_ref[group]
    values[:, HD : 2 * HD] = jnp.ones((values.shape[0], HD), jnp.bfloat16)
    for block in range(RING):
        held = query_ref[block]
        for head in range(HEADS):
            at = block * ROWS + head * CS
            rows[at : at + CS, 0:HD] = held[:, head * HD : (head + 1) * HD]
            rows[at : at + CS, HD : 2 * HD] = held[:, HEADS * HD : (HEADS + 1) * HD]

    lower = -1
    for tokens in SIZES:

        @pl.when((filled * PAGE > lower) & (filled * PAGE <= tokens))
        def run(tokens=tokens):
            def one_blank(page, carry):
                target = pl.ds(pl.multiple_of(page * PAGE, PAGE), PAGE)
                keys[target, 0:HD] = jnp.zeros((PAGE, HD), jnp.bfloat16)
                keys[target, HD : 2 * HD] = jnp.full((PAGE, HD), -BIG, jnp.bfloat16)
                values[target, 0:HD] = jnp.zeros((PAGE, HD), jnp.bfloat16)
                return carry

            lax.fori_loop(filled, tokens // PAGE, one_blank, 0)
            attend_tokens(tokens, rows, keys, values, levels, out_ref)

        lower = tokens
    diagonal = lax.broadcasted_iota(jnp.int32, (HD, HD), 0) == lax.broadcasted_iota(jnp.int32, (HD, HD), 1)
    for block in range(RING):
        level = levels[block * ROWS : (block + 1) * ROWS, :]
        lines = [
            jnp.sum(jnp.where(diagonal, level[half * HD : (half + 1) * HD], 0.0), axis=0, keepdims=True)
            for half in range(2)
        ]
        line = jnp.concatenate(lines, axis=0)
        high = line.astype(jnp.bfloat16).astype(jnp.float32)
        middle = (line - high).astype(jnp.bfloat16).astype(jnp.float32)
        low = line - high - middle
        tail = jnp.concatenate([high, middle, low, jnp.zeros((10, HD), jnp.float32)], axis=0)
        out_ref[block, ROWS : ROWS + 16, :] = tail.astype(jnp.bfloat16)


def attend(pages, used, query, pool, count):
    tokens = (GROUPS * PAGES_DEV + UNROLL) * PAGE
    vmem = pl.BlockSpec(memory_space=pltpu.VMEM)
    smem = pl.BlockSpec(memory_space=pltpu.SMEM)
    return pl.pallas_call(
        attend_kernel,
        out_shape=jax.ShapeDtypeStruct((RING, ROWS + 16, HD), jnp.bfloat16),
        in_specs=[smem, smem] + [vmem] * 10,
        out_specs=vmem,
        scratch_shapes=[
            pltpu.VMEM((tokens, 2 * HD), jnp.bfloat16),
            pltpu.VMEM((tokens, 2 * HD), jnp.bfloat16),
            pltpu.VMEM((RING * ROWS, 2 * HD), jnp.bfloat16),
            pltpu.VMEM((RING * ROWS, HD), jnp.float32),
        ],
        cost_estimate=cost(10.0),
        compiler_params=pltpu.CompilerParams(vmem_limit_bytes=40 * MIB),
        name="attend",
    )(pages, used, query, *pool, count)


def finish_kernel(
    parts_ref, query_ref, key_ref, value_ref, allowed_ref, alive_ref, weight_ref, out_ref, weights, ready
):
    width = out_ref.shape[2]
    copies = [
        pltpu.make_async_copy(
            weight_ref.at[:, part * width : (part + 1) * width], weights.at[part], ready.at[part]
        )
        for part in range(out_ref.shape[0])
    ]
    for copy in copies:
        copy.start()
    diagonal = lax.broadcasted_iota(jnp.int32, (HD, HD), 0) == lax.broadcasted_iota(jnp.int32, (HD, HD), 1)
    levels = []
    for block in range(RING):
        tail = parts_ref[block, ROWS : ROWS + 16, :].astype(jnp.float32)
        line = tail[0:2] + tail[2:4] + tail[4:6]
        columns = [
            jnp.sum(jnp.where(diagonal, jnp.broadcast_to(line[half : half + 1], (HD, HD)), 0.0), axis=1, keepdims=True)
            for half in range(2)
        ]
        levels.append(jnp.concatenate(columns, axis=0))
    query = jnp.concatenate([query_ref[0, :, head * HD : (head + 1) * HD] for head in range(HEADS)], axis=0)
    scores = lax.dot_general(
        query, key_ref[...], (((1,), (1,)), ((), ())), preferred_element_type=jnp.float32
    )
    allowed = jnp.concatenate([allowed_ref[...]] * HEADS, axis=0) > 0
    scores = jnp.where(allowed, scores * C2, -BIG)
    own_top = jnp.max(scores, axis=1, keepdims=True)
    own = jnp.where(allowed, jnp.exp2(scores - own_top), 0.0)
    own_sum = jnp.dot(own.astype(jnp.bfloat16), value_ref[...], preferred_element_type=jnp.float32)
    best = own_top
    for level in levels:
        best = jnp.maximum(best, level)
    factor = jnp.exp2(own_top - best)
    total = factor * jnp.sum(own, axis=1, keepdims=True)
    summed = factor * own_sum
    for block in range(RING):
        factor = jnp.exp2(levels[block] - best)
        total = total + factor
        summed = summed + factor * parts_ref[block, 0:ROWS, :].astype(jnp.float32)
    result = (summed / total).astype(jnp.bfloat16)
    attended = jnp.concatenate([result[head * CS : (head + 1) * CS, :] for head in range(HEADS)], axis=1)

    for part, copy in enumerate(copies):
        copy.wait()
        terms = jnp.dot(attended, weights[part], preferred_element_type=jnp.float32)
        out_ref[part] = (terms * alive_ref[...]).astype(jnp.bfloat16)


def finish(parts, query, keys, values, allowed, alive, weight):
    blocks = 8
    width = weight.shape[1] // blocks
    vmem = pl.BlockSpec(memory_space=pltpu.VMEM)
    return pl.pallas_call(
        finish_kernel,
        out_shape=jax.ShapeDtypeStruct((blocks, CS, width), jnp.bfloat16),
        in_specs=[vmem] * 6 + [pl.BlockSpec(memory_space=pltpu.HBM)],
        out_specs=vmem,
        scratch_shapes=[
            pltpu.VMEM((blocks, weight.shape[0], width), jnp.bfloat16),
            pltpu.SemaphoreType.DMA((blocks,)),
        ],
        cost_estimate=cost(4.0),
        compiler_params=pltpu.CompilerParams(vmem_limit_bytes=57 * MIB),
        name="finish",
    )(parts, query, keys, values, allowed, alive, weight)


def body(
    queries, new_keys, new_values, pool_keys, pool_values, out_weight, page_table, prefix_len, parent, finished
):
    children, steps, width = queries.shape
    rows = children * steps
    nodes, path_pages = page_table.shape
    sent = prepare(parent, queries)
    gathered = lax.all_to_all(sent, "z", split_axis=0, concat_axis=0, tiled=True)

    pool_values, sent = lax.optimization_barrier((pool_values, sent))

    def swap(values, axis):
        return [lax.ppermute(value, axis, [(0, 1), (1, 0)]) for value in values]

    kv = [pool_keys, pool_values]
    kv_far = swap(kv, "yh")
    kv_core = swap(kv, "c")
    yh, z, core = lax.axis_index("yh"), lax.axis_index("z"), lax.axis_index("c")
    first = jnp.stack(
        [
            PAGES_DEV * ((a * RING + z) * 2 + b)
            for a, b in ((yh, core), (yh, 1 - core), (1 - yh, core), (1 - yh, 1 - core))
        ]
    ).astype(jnp.int32)
    table = page_table.T.reshape(nodes * path_pages // HD, HD)
    place = jnp.arange(path_pages, dtype=jnp.int32)
    left = jnp.clip(prefix_len[None, :] - PAGE * place[:, None], 0, PAGE).reshape(table.shape)
    count = path_masks(first, table, left)
    kv_far[0], kv_far[1], count = lax.optimization_barrier((kv_far[0], kv_far[1], count))
    kv_far_core = swap(kv_far, "c")
    taken = jnp.any(count[:, :nodes] > 0, axis=1).reshape(GROUPS, PAGES_DEV)
    order = jnp.arange(PAGES_DEV, dtype=jnp.int32)
    earlier = taken[:, None, :] & (order[None, None, :] < order[None, :, None])
    rank = jnp.sum(earlier.astype(jnp.int32), axis=2)
    chosen = taken[:, :, None] & (rank[:, :, None] == order[None, None, :])
    pages = jnp.sum(jnp.where(chosen, order[None, :, None], 0), axis=1).reshape(GROUPS * PAGES_DEV)
    used = jnp.sum(taken.astype(jnp.int32), axis=1)
    parts = attend(pages, used, gathered, kv + kv_core + kv_far + kv_far_core, count)
    parts = lax.all_to_all(parts, "z", split_axis=0, concat_axis=0, tiled=True)

    alive = 1 - finished
    child = jnp.arange(rows, dtype=jnp.int32) // steps
    step = jnp.arange(rows, dtype=jnp.int32) % steps
    allowed = (
        (child[:, None] == child[None, :])
        & (step[None, :] <= step[:, None])
        & (alive.reshape(1, rows) > 0)
    ).astype(jnp.int32)
    terms = finish(
        parts,
        sent,
        new_keys.reshape(rows, HD),
        new_values.reshape(rows, HD),
        allowed,
        alive.reshape(rows, 1).astype(jnp.float32),
        out_weight,
    )
    terms = lax.all_to_all(terms, ("yl", "x"), split_axis=0, concat_axis=0, tiled=True)
    return jnp.sum(terms.astype(jnp.float32), axis=0).reshape(children, steps, terms.shape[-1])


def solution(mesh):
    fine = Mesh(mesh.devices.reshape(2, RING, 2, 2, 4), ("yh", "z", "c", "yl", "x"))
    branch, tensor = ("yh", "z", "c"), ("yl", "x")
    placed = (
        P(branch, None, tensor),
        P(branch, None, tensor),
        P(branch, None, tensor),
        P(branch, None, tensor),
        P(branch, None, tensor),
        P(tensor, None),
        P(),
        P(),
        P(branch),
        P(branch, None),
    )
    return jax.shard_map(
        body, mesh=fine, in_specs=placed, out_specs=P(branch, None, tensor), check_vma=False
    )
```

time: 95.6 us -> 84.6 us (0.88)
  starting transfers between devices: 20.8 us -> 16 us
  local copies, waits for them, and re-layouts: 9.03 us -> 4.7 us
  waiting for transfers between devices: 26.6 us -> 23.2 us
  Pallas kernels: 23 us -> 24.3 us
  blocking collectives: 12.3 us -> 13.4 us
  other arithmetic: 2.53 us -> 1.47 us
    all_to_all x1, starting transfers between devices: 11.9 us -> 3.54 us  [body(): parts = lax.all_to_all(parts, 'z', split_axis=0, concat_axis=0, tiled=True)]
    ppermute x3 -> x6, waiting for transfers between devices: 8.17 us -> 1.99 us  [swap(): return [lax.ppermute(value, axis, [(0, 1), (1, 0)]) for value in values]]
    all_to_all x1, waiting for transfers between devices: 0.01 us -> 4.24 us  [body(): lax.all_to_all(sent, 'z', split_axis=0, concat_axis=0, tiled=True)]
    ppermute x3 -> x6, starting transfers between devices: 2.16 us -> 5.78 us  [swap(): return [lax.ppermute(value, axis, [(0, 1), (1, 0)]) for value in values]]
    pallas_call x2 -> x3, Pallas kernels: 11.1 us -> 14.1 us  [the longest x1 6.56 us: path_masks(): pl.pallas_call(mask_kernel, out_shape=jax.ShapeDtypeStruct((GROUPS * PAGE...]
    unnamed x8, local copies, waits for them, and re-layouts: 3.4 us -> 0.82 us
    pallas_call x1, Pallas kernels: 11.9 us -> 10.2 us  [attend(): pl.pallas_call(attend_kernel, out_shape=jax.ShapeDtypeStruct((RING, ROWS...]
    broadcast_in_dim x2 -> x0, local copies, waits for them, and re-layouts: 1.58 us -> none  [the longest x1 0.86 us: body(): jnp.broadcast_to(sent[None], (RING,) + sent.shape)]
  transfers between devices with their start and end apart: 5 -> 8, of which waited for: 2 -> 5; matrix products, arithmetic and copies ran while one was open for 7% -> 6% of each run, Pallas kernels for 8% -> 8%
where the time goes in v2:
time: 84.6 us; the launch traced here: 83.2 us
  Pallas kernels  24.3 us (29%)
  waiting for transfers between devices  23.2 us (27%)
  starting transfers between devices  16 us (19%)
  blocking collectives  13.4 us (16%)
  local copies, waits for them, and re-layouts  4.7 us (6%)
  other arithmetic  1.47 us (2%)
    all_to_all x1, waiting for transfers between devices, body(): parts = lax.all_to_all(parts, 'z', split_axis=0, concat_axis=0, tiled=True)  17 us
    all_to_all x1, blocking collectives, body(): lax.all_to_all(terms, ('yl', 'x'), split_axis=0, concat_axis=0, tiled=True)  13.4 us
    pallas_call x1, Pallas kernels, attend(): pl.pallas_call(attend_kernel, out_shape=jax.ShapeDtypeStruct((RING, ROWS...  10.2 us
    all_to_all x1, starting transfers between devices, body(): lax.all_to_all(sent, 'z', split_axis=0, concat_axis=0, tiled=True)  6.73 us
    pallas_call x1, Pallas kernels, path_masks(): pl.pallas_call(mask_kernel, out_shape=jax.ShapeDtypeStruct((GROUPS * PAGE...  6.56 us
    ppermute x6, starting transfers between devices, swap(): return [lax.ppermute(value, axis, [(0, 1), (1, 0)]) for value in values]  5.78 us
    pallas_call x1, Pallas kernels, finish(): pl.pallas_call(finish_kernel, out_shape=jax.ShapeDtypeStruct((blocks, CS,...  5.78 us
    all_to_all x1, waiting for transfers between devices, body(): lax.all_to_all(sent, 'z', split_axis=0, concat_axis=0, tiled=True)  4.24 us
  transfers between devices with their start and end apart: 8, of which 5 were waited for; matrix products, arithmetic and copies ran while one was open for 6% of the time, Pallas kernels for 8%

profile of v2, /device:TPU:16, one launch (start us, length us, event | category | flops | bytes accessed | tf_op | source)
XLA Modules:
  0.0 83.2 jit_solution(6069110444231716904)
XLA Ops:
  0.0 1.7 %prepare.1.query_ref = bf16[8,32,1152]{2,1,0:T(8,128)(2,1)} custom-call(s32[8]{0:T(128)} %parent_ref.1, bf16[8,4,1024]{2,1,0:T(4,128)(2,1)} %query_ref.1), custom_call_target="tpu_custom_call" | custom-call | flops 1150000000 | bytes 65536 | tf_op jit(solution)/shard_map/prepare/pallas_call | solution.py:42
  1.7 2.1 %collective-permute-start.1 = (bf16[96,16,128]{2,1,0:T(8,128)(2,1)}, bf16[96,16,128]{2,1,0:T(8,128)(2,1)S(1)}, u32[]{:S(2)}, u32[]{:S(2)}) collective-permute-start(bf16[96,16,128]{2,1,0:T(8,128)(2,1)} %va_ref), channel_id=1, source_target_pairs={{0,128},{128,0},{1,129},{129,1},{2,130},{130,2},{3,131},{131,3},{4... | collective-permute-start | bytes 1179656 | tf_op jit(solution)/shard_map/ppermute | solution.py:283
  3.8 0.0 collective-permute-start.3
  3.8 6.7 %all-to-all-start = ((bf16[8,32,1152]{2,1,0:T(8,128)(2,1)}), bf16[8,32,1152]{2,1,0:T(8,128)(2,1)S(1)}, u32[]{:S(2)}, u32[]{:S(2)}) async-start(bf16[8,32,1152]{2,1,0:T(8,128)(2,1)} %prepare.1.query_ref), calls=%async_computation | async-start | bytes 1179648 | tf_op jit(solution)/shard_map/all_to_all | solution.py:278
  10.5 3.2 %collective-permute-start = (bf16[96,16,128]{2,1,0:T(8,128)(2,1)}, bf16[96,16,128]{2,1,0:T(8,128)(2,1)S(1)}, u32[]{:S(2)}, u32[]{:S(2)}) collective-permute-start(bf16[96,16,128]{2,1,0:T(8,128)(2,1)} %ka_ref.1), channel_id=1, source_target_pairs={{0,128},{128,0},{1,129},{129,1},{2,130},{130,2},{3,131},{131,3},{4... | collective-permute-start | bytes 1179656 | tf_op jit(solution)/shard_map/ppermute | solution.py:283
  13.7 0.0 collective-permute-start.2
  13.7 1.1 %copy.20 = s32[1024,32]{1,0:T(8,128)S(1)} copy(s32[1024,32]{0,1:T(8,128)} %bitcast.9) | data formatting | bytes 262144 | tf_op jit(solution)/shard_map/transpose | solution.py:295
  14.8 0.2 reshape.113.table_ref
  15.0 0.1 copy.21
  15.1 0.7 sub.42
  15.8 0.1 sub.43
  15.9 0.1 pad_add_fusion.first_ref
  16.0 0.0 copy-start
  16.0 0.0 copy-start.1
  16.0 6.6 %path_masks.1.count_ref = s32[384,128]{1,0:T(8,128)S(1)} custom-call(s32[4]{0:T(128)S(1)} %pad_add_fusion.first_ref, s32[256,128]{1,0:T(8,128)S(1)} %reshape.113.table_ref, s32[256,128]{1,0:T(8,128)S(1)} %subtract_clamp_fusion.left_ref), custom_call_target="tpu_custom_call" | custom-call | flops 8049999872 | bytes 65536 | tf_op jit(solution)/shard_map/path_masks/pallas_call | solution.py:71
  22.6 0.0 collective-permute-done.1.vc_ref
  22.6 0.9 %collective-permute-done.kc_ref = bf16[96,16,128]{2,1,0:T(8,128)(2,1)S(1)} collective-permute-done((bf16[96,16,128]{2,1,0:T(8,128)(2,1)}, bf16[96,16,128]{2,1,0:T(8,128)(2,1)S(1)}, u32[]{:S(2)}, u32[]{:S(2)}) %collective-permute-start) | collective-permute-done | bytes 393248 | tf_op jit(solution)/shard_map/ppermute | solution.py:283
  23.5 0.0 collective-permute-start.4
  23.5 0.5 collective-permute-start.5
  24.0 0.1 fusion
  24.2 0.1 and.78
  24.2 0.2 convert_reduce_fusion.1
  24.4 0.2 select_reduce_fusion
  24.6 0.1 reshape.114.list_ref
  24.7 0.1 convert_reduce_fusion.2.used_ref
  24.8 0.0 copy-start.3
  24.8 0.0 collective-permute-done.3.vb_ref
  24.8 0.0 collective-permute-done.2.kb_ref
  24.8 0.5 collective-permute-done.4.kd_ref
  25.4 0.6 collective-permute-done.5.vd_ref
  25.9 4.2 %all-to-all-done.query_ref = bf16[8,32,1152]{2,1,0:T(8,128)(2,1)S(1)} async-done(((bf16[8,32,1152]{2,1,0:T(8,128)(2,1)}), bf16[8,32,1152]{2,1,0:T(8,128)(2,1)S(1)}, u32[]{:S(2)}, u32[]{:S(2)}) %all-to-all-start) | async-done | bytes 589856 | tf_op jit(solution)/shard_map/all_to_all | solution.py:278
  30.2 0.0 copy-done
  30.2 0.0 copy-done.1
  30.2 10.2 %attend.1 = bf16[8,272,128]{2,1,0:T(8,128)(2,1)} custom-call(s32[384]{0:T(512)S(1)} %reshape.114.list_ref, s32[4]{0:T(128)S(1)} %convert_reduce_fusion.2.used_ref, bf16[8,32,1152]{2,1,0:T(8,128)(2,1)S(1)} %all-to-all-done.query_ref, bf16[96,16,128]{2,1,0:T(8,128)(2,1)S(1)} %copy-done, bf16[96,16,128]{2,1,0:T(8,128)(2,1)S(1)} %copy-done.1, ...), custom_call_target="tpu_custom_call" | custom-call | flops 11500000256 | bytes 65536 | tf_op jit(solution)/shard_map/attend/pallas_call | solution.py:185
  40.4 3.5 %all-to-all-start.1 = ((bf16[8,272,128]{2,1,0:T(8,128)(2,1)}), bf16[8,272,128]{2,1,0:T(8,128)(2,1)S(1)}, u32[]{:S(2)}, u32[]{:S(2)}) async-start(bf16[8,272,128]{2,1,0:T(8,128)(2,1)} %attend.1), calls=%async_computation.1 | async-start | bytes 1114112 | tf_op jit(solution)/shard_map/all_to_all | solution.py:309
  43.9 0.0 copy-done.3
  43.9 0.1 copy.22
  44.0 0.1 gt.21
  44.1 0.1 copy.23
  44.2 0.7 convert_element_type.23.alive_ref
  44.9 0.7 and_convert_fusion.allowed_ref
  45.6 17.0 %all-to-all-done.1.parts_ref = bf16[8,272,128]{2,1,0:T(8,128)(2,1)S(1)} async-done(((bf16[8,272,128]{2,1,0:T(8,128)(2,1)}), bf16[8,272,128]{2,1,0:T(8,128)(2,1)S(1)}, u32[]{:S(2)}, u32[]{:S(2)}) %all-to-all-start.1) | async-done | bytes 557088 | tf_op jit(solution)/shard_map/all_to_all | solution.py:309
  62.6 0.0 copy-start.2
  62.6 0.8 copy-done.2
  63.4 5.8 %finish.1 = bf16[8,32,512]{2,1,0:T(8,128)(2,1)} custom-call(bf16[8,272,128]{2,1,0:T(8,128)(2,1)} %copy-done.2, bf16[8,32,1152]{2,1,0:T(8,128)(2,1)} %prepare.1.query_ref, bf16[32,128]{1,0:T(8,128)(2,1)} %bitcast.10, bf16[32,128]{1,0:T(8,128)(2,1)} %bitcast.11, s32[32,32]{1,0:T(8,128)} %and_convert_fusion.allowed_ref, ...), custom_call_target="tpu_custom_call" | custom-call | flops 4600000000 | bytes 65536 | tf_op jit(solution)/shard_map/finish/pallas_call | solution.py:256
  69.1 13.4 %all_to_all.15 = bf16[8,32,512]{2,1,0:T(8,128)(2,1)S(1)} all-to-all(bf16[8,32,512]{2,1,0:T(8,128)(2,1)} %finish.1), channel_id=1, replica_groups=mesh['yh'=2,'z'=8,'c'=2,'yl'=2,'x'=4] {'yl','x'}, dimensions={0} | all-to-all | bytes 524288 | tf_op jit(solution)/shard_map/all_to_all | solution.py:328
  82.6 0.7 reshape.117
  (8 shorter events, 0.1 us)
Async XLA Ops:
  1.7 20.9 %collective-permute-start.1 = (bf16[96,16,128]{2,1,0:T(8,128)(2,1)}, bf16[96,16,128]{2,1,0:T(8,128)(2,1)S(1)}, u32[]{:S(2)}, u32[]{:S(2)}) collective-permute-start(bf16[96,16,128]{2,1,0:T(8,128)(2,1)} %va_ref), channel_id=1, source_target_pairs={{0,128},{128,0},{1,129},{129,1},{2,130},{130,2},{3,131},{131,3},{4... | collective-permute-start | bytes 1179656 | tf_op jit(solution)/shard_map/ppermute | solution.py:283
  3.8 21.0 %collective-permute-start.3 = (bf16[96,16,128]{2,1,0:T(8,128)(2,1)}, bf16[96,16,128]{2,1,0:T(8,128)(2,1)S(1)}, u32[]{:S(2)}, u32[]{:S(2)}) collective-permute-start(bf16[96,16,128]{2,1,0:T(8,128)(2,1)} %va_ref), channel_id=1, source_target_pairs={{0,8},{8,0},{1,9},{9,1},{2,10},{10,2},{3,11},{11,3},{4,12},{12,4},... | collective-permute-start | bytes 1179656 | tf_op jit(solution)/shard_map/ppermute | solution.py:283
  3.8 26.3 %all-to-all-start = ((bf16[8,32,1152]{2,1,0:T(8,128)(2,1)}), bf16[8,32,1152]{2,1,0:T(8,128)(2,1)S(1)}, u32[]{:S(2)}, u32[]{:S(2)}) async-start(bf16[8,32,1152]{2,1,0:T(8,128)(2,1)} %prepare.1.query_ref), calls=%async_computation | async-start | bytes 1179648 | tf_op jit(solution)/shard_map/all_to_all | solution.py:278
  10.5 13.0 %collective-permute-start = (bf16[96,16,128]{2,1,0:T(8,128)(2,1)}, bf16[96,16,128]{2,1,0:T(8,128)(2,1)S(1)}, u32[]{:S(2)}, u32[]{:S(2)}) collective-permute-start(bf16[96,16,128]{2,1,0:T(8,128)(2,1)} %ka_ref.1), channel_id=1, source_target_pairs={{0,128},{128,0},{1,129},{129,1},{2,130},{130,2},{3,131},{131,3},{4... | collective-permute-start | bytes 1179656 | tf_op jit(solution)/shard_map/ppermute | solution.py:283
  13.7 11.1 %collective-permute-start.2 = (bf16[96,16,128]{2,1,0:T(8,128)(2,1)}, bf16[96,16,128]{2,1,0:T(8,128)(2,1)S(1)}, u32[]{:S(2)}, u32[]{:S(2)}) collective-permute-start(bf16[96,16,128]{2,1,0:T(8,128)(2,1)} %ka_ref.1), channel_id=1, source_target_pairs={{0,8},{8,0},{1,9},{9,1},{2,10},{10,2},{3,11},{11,3},{4,12},{12,4},... | collective-permute-start | bytes 1179656 | tf_op jit(solution)/shard_map/ppermute | solution.py:283
  16.0 14.2 %copy-start = (bf16[96,16,128]{2,1,0:T(8,128)(2,1)S(1)}, bf16[96,16,128]{2,1,0:T(8,128)(2,1)}, u32[]{:S(2)}) copy-start(bf16[96,16,128]{2,1,0:T(8,128)(2,1)} %ka_ref.1) | copy-start | bytes 1179652
  16.0 14.2 %copy-start.1 = (bf16[96,16,128]{2,1,0:T(8,128)(2,1)S(1)}, bf16[96,16,128]{2,1,0:T(8,128)(2,1)}, u32[]{:S(2)}) copy-start(bf16[96,16,128]{2,1,0:T(8,128)(2,1)} %va_ref) | copy-start | bytes 1179652
  23.5 1.9 %collective-permute-start.4 = (bf16[96,16,128]{2,1,0:T(8,128)(2,1)S(1)}, bf16[96,16,128]{2,1,0:T(8,128)(2,1)}, u32[]{:S(2)}, u32[]{:S(2)}) collective-permute-start(bf16[96,16,128]{2,1,0:T(8,128)(2,1)S(1)} %collective-permute-done.kc_ref), channel_id=1, source_target_pairs={{0,8},{8,0},{1,9},{9,1},{2,10},{10,2},{3,11},{11,3},{4,12},{12,4},... | collective-permute-start | bytes 1179656 | tf_op jit(solution)/shard_map/ppermute | solution.py:283
  23.5 2.4 %collective-permute-start.5 = (bf16[96,16,128]{2,1,0:T(8,128)(2,1)S(1)}, bf16[96,16,128]{2,1,0:T(8,128)(2,1)}, u32[]{:S(2)}, u32[]{:S(2)}) collective-permute-start(bf16[96,16,128]{2,1,0:T(8,128)(2,1)S(1)} %collective-permute-done.1.vc_ref), channel_id=1, source_target_pairs={{0,8},{8,0},{1,9},{9,1},{2,10},{10,2},{3,11},{11,3},{4,12},{12,4},... | collective-permute-start | bytes 1179656 | tf_op jit(solution)/shard_map/ppermute | solution.py:283
  24.8 19.1 %copy-start.3 = (s32[8,4]{0,1:T(4,128)S(1)}, s32[8,4]{0,1:T(4,128)}, u32[]{:S(2)}) copy-start(s32[8,4]{0,1:T(4,128)} %param.19) | copy-start | bytes 388
  40.4 22.2 %all-to-all-start.1 = ((bf16[8,272,128]{2,1,0:T(8,128)(2,1)}), bf16[8,272,128]{2,1,0:T(8,128)(2,1)S(1)}, u32[]{:S(2)}, u32[]{:S(2)}) async-start(bf16[8,272,128]{2,1,0:T(8,128)(2,1)} %attend.1), calls=%async_computation.1 | async-start | bytes 1114112 | tf_op jit(solution)/shard_map/all_to_all | solution.py:309
  62.6 0.8 copy-start.2

commit v3 on v2

--- a/solution.py
+++ b/solution.py
@@ -84,8 +84,10 @@
 
 
 def attend_tokens(tokens, rows, keys, values, levels, out_ref):
+    chunk = 2 * ROWS if tokens < 3000 else ROWS
+
     def span(block):
-        return pl.ds(pl.multiple_of(block * ROWS, ROWS), ROWS)
+        return pl.ds(pl.multiple_of(block * chunk, chunk), chunk)
 
     def score(block):
         return lax.dot_general(
@@ -100,7 +102,9 @@
     def store(block, top, weights):
         summed = jnp.dot(weights, values[0:tokens, :], preferred_element_type=jnp.float32)
         total = summed[:, HD : 2 * HD]
-        out_ref[block, 0:ROWS, :] = (summed[:, 0:HD] / total).astype(jnp.bfloat16)
+        result = (summed[:, 0:HD] / total).astype(jnp.bfloat16)
+        for part in range(chunk // ROWS):
+            out_ref[block * (chunk // ROWS) + part, 0:ROWS, :] = result[part * ROWS : (part + 1) * ROWS]
         levels[span(block), :] = top + jnp.log2(total)
 
     def some_blocks(step, carry):
@@ -115,7 +119,7 @@
         store(*held)
         return carry
 
-    lax.fori_loop(0, RING // TOGETHER, some_blocks, 0)
+    lax.fori_loop(0, RING * ROWS // chunk // TOGETHER, some_blocks, 0)
 
 
 def attend_kernel(
@@ -194,23 +198,38 @@
             pltpu.VMEM((RING * ROWS, HD), jnp.float32),
         ],
         cost_estimate=cost(10.0),
-        compiler_params=pltpu.CompilerParams(vmem_limit_bytes=40 * MIB),
+        compiler_params=pltpu.CompilerParams(vmem_limit_bytes=30 * MIB),
         name="attend",
     )(pages, used, query, *pool, count)
 
 
+def permit_kernel(finished_ref, allowed_ref, alive_ref):
+    row = lax.broadcasted_iota(jnp.int32, (CS, HD), 0)
+    column = lax.broadcasted_iota(jnp.int32, (CS, HD), 1)
+    same = (row // 4 == column // 4) & (column <= row)
+    alive = 1 - finished_ref[...]
+    allowed_ref[...] = jnp.where(same, jnp.broadcast_to(alive, (CS, HD)), 0)
+    own = jnp.where(row == column, jnp.broadcast_to(alive, (CS, HD)), 0)
+    alive_ref[...] = jnp.broadcast_to(jnp.sum(own, axis=1, keepdims=True), (CS, HD)).astype(jnp.float32)
+
+
+def permit(finished):
+    vmem = pl.BlockSpec(memory_space=pltpu.VMEM)
+    return pl.pallas_call(
+        permit_kernel,
+        out_shape=(jax.ShapeDtypeStruct((CS, HD), jnp.int32), jax.ShapeDtypeStruct((CS, HD), jnp.float32)),
+        in_specs=[vmem],
+        out_specs=(vmem, vmem),
+        cost_estimate=cost(15.0),
+        compiler_params=pltpu.CompilerParams(vmem_limit_bytes=2 * MIB),
+        name="permit",
+    )(finished)
+
+
 def finish_kernel(
-    parts_ref, query_ref, key_ref, value_ref, allowed_ref, alive_ref, weight_ref, out_ref, weights, ready
+    parts_ref, query_ref, key_ref, value_ref, allowed_ref, alive_ref, weight_ref, out_ref
 ):
     width = out_ref.shape[2]
-    copies = [
-        pltpu.make_async_copy(
-            weight_ref.at[:, part * width : (part + 1) * width], weights.at[part], ready.at[part]
-        )
-        for part in range(out_ref.shape[0])
-    ]
-    for copy in copies:
-        copy.start()
     diagonal = lax.broadcasted_iota(jnp.int32, (HD, HD), 0) == lax.broadcasted_iota(jnp.int32, (HD, HD), 1)
     levels = []
     for block in range(RING):
@@ -225,7 +244,7 @@
     scores = lax.dot_general(
         query, key_ref[...], (((1,), (1,)), ((), ())), preferred_element_type=jnp.float32
     )
-    allowed = jnp.concatenate([allowed_ref[...]] * HEADS, axis=0) > 0
+    allowed = jnp.concatenate([allowed_ref[:, 0:CS]] * HEADS, axis=0) > 0
     scores = jnp.where(allowed, scores * C2, -BIG)
     own_top = jnp.max(scores, axis=1, keepdims=True)
     own = jnp.where(allowed, jnp.exp2(scores - own_top), 0.0)
@@ -243,10 +262,10 @@
     result = (summed / total).astype(jnp.bfloat16)
     attended = jnp.concatenate([result[head * CS : (head + 1) * CS, :] for head in range(HEADS)], axis=1)
 
-    for part, copy in enumerate(copies):
-        copy.wait()
-        terms = jnp.dot(attended, weights[part], preferred_element_type=jnp.float32)
-        out_ref[part] = (terms * alive_ref[...]).astype(jnp.bfloat16)
+    for part in range(out_ref.shape[0]):
+        columns = weight_ref[:, part * width : (part + 1) * width]
+        terms = jnp.dot(attended, columns, preferred_element_type=jnp.float32)
+        out_ref[part] = (terms * alive_ref[:, 0:1]).astype(jnp.bfloat16)
 
 
 def finish(parts, query, keys, values, allowed, alive, weight):
@@ -256,14 +275,10 @@
     return pl.pallas_call(
         finish_kernel,
         out_shape=jax.ShapeDtypeStruct((blocks, CS, width), jnp.bfloat16),
-        in_specs=[vmem] * 6 + [pl.BlockSpec(memory_space=pltpu.HBM)],
+        in_specs=[vmem] * 7,
         out_specs=vmem,
-        scratch_shapes=[
-            pltpu.VMEM((blocks, weight.shape[0], width), jnp.bfloat16),
-            pltpu.SemaphoreType.DMA((blocks,)),
-        ],
         cost_estimate=cost(4.0),
-        compiler_params=pltpu.CompilerParams(vmem_limit_bytes=57 * MIB),
+        compiler_params=pltpu.CompilerParams(vmem_limit_bytes=12 * MIB),
         name="finish",
     )(parts, query, keys, values, allowed, alive, weight)
 
@@ -277,14 +292,13 @@
     sent = prepare(parent, queries)
     gathered = lax.all_to_all(sent, "z", split_axis=0, concat_axis=0, tiled=True)
 
-    pool_values, sent = lax.optimization_barrier((pool_values, sent))
-
     def swap(values, axis):
         return [lax.ppermute(value, axis, [(0, 1), (1, 0)]) for value in values]
 
     kv = [pool_keys, pool_values]
     kv_far = swap(kv, "yh")
-    kv_core = swap(kv, "c")
+    near_keys, near_values, sent = lax.optimization_barrier((pool_keys, pool_values, sent))
+    kv_core = swap([near_keys, near_values], "c")
     yh, z, core = lax.axis_index("yh"), lax.axis_index("z"), lax.axis_index("c")
     first = jnp.stack(
         [
@@ -306,23 +320,18 @@
     pages = jnp.sum(jnp.where(chosen, order[None, :, None], 0), axis=1).reshape(GROUPS * PAGES_DEV)
     used = jnp.sum(taken.astype(jnp.int32), axis=1)
     parts = attend(pages, used, gathered, kv + kv_core + kv_far + kv_far_core, count)
+    line = jnp.pad(finished.reshape(1, rows), ((0, 0), (0, HD - rows)), constant_values=1)
+    parts, line = lax.optimization_barrier((parts, line))
+    allowed, alive = permit(line)
     parts = lax.all_to_all(parts, "z", split_axis=0, concat_axis=0, tiled=True)
 
-    alive = 1 - finished
-    child = jnp.arange(rows, dtype=jnp.int32) // steps
-    step = jnp.arange(rows, dtype=jnp.int32) % steps
-    allowed = (
-        (child[:, None] == child[None, :])
-        & (step[None, :] <= step[:, None])
-        & (alive.reshape(1, rows) > 0)
-    ).astype(jnp.int32)
     terms = finish(
         parts,
         sent,
         new_keys.reshape(rows, HD),
         new_values.reshape(rows, HD),
         allowed,
-        alive.reshape(rows, 1).astype(jnp.float32),
+        alive,
         out_weight,
     )
     terms = lax.all_to_all(terms, ("yl", "x"), split_axis=0, concat_axis=0, tiled=True)

time: 84.6 us -> 81 us (0.957); the launches traced: 83.2 us -> 80.6 us
  Pallas kernels: 24.3 us -> 20 us
  local copies, waits for them, and re-layouts: 4.7 us -> 6.51 us
  blocking collectives: 13.4 us -> 12.1 us
  waiting for transfers between devices: 23.2 us -> 24.5 us
    pallas_call x1, Pallas kernels: 5.78 us -> 2.21 us  [finish(): pl.pallas_call(finish_kernel, out_shape=jax.ShapeDtypeStruct((blocks, CS,...]
    unnamed x8 -> x15, local copies, waits for them, and re-layouts: 0.82 us -> 3.49 us
    all_to_all x1, waiting for transfers between devices: 4.24 us -> 6.26 us  [body(): lax.all_to_all(sent, 'z', split_axis=0, concat_axis=0, tiled=True)]
    all_to_all x1, starting transfers between devices: 6.73 us -> 8.47 us  [body(): lax.all_to_all(sent, 'z', split_axis=0, concat_axis=0, tiled=True)]
    all_to_all x1, blocking collectives: 13.4 us -> 12.1 us  [body(): lax.all_to_all(terms, ('yl', 'x'), split_axis=0, concat_axis=0, tiled=True)]
    ppermute x6, starting transfers between devices: 5.78 us -> 4.63 us  [swap(): return [lax.ppermute(value, axis, [(0, 1), (1, 0)]) for value in values]]
    ppermute x6, waiting for transfers between devices: 1.99 us -> 1.11 us  [swap(): return [lax.ppermute(value, axis, [(0, 1), (1, 0)]) for value in values]]
  transfers between devices with their start and end apart: 8 -> 8, of which waited for: 5 -> 4; matrix products, arithmetic and copies ran while one was open for 6% -> 4% of each run, Pallas kernels for 8% -> 10%
where the time goes in v3:
time: 81 us; the launch traced here: 80.6 us
  waiting for transfers between devices  24.5 us (30%)
  Pallas kernels  20 us (25%)
  starting transfers between devices  16.6 us (20%)
  blocking collectives  12.1 us (15%)
  local copies, waits for them, and re-layouts  6.51 us (8%)
    all_to_all x1, waiting for transfers between devices, body(): parts = lax.all_to_all(parts, 'z', split_axis=0, concat_axis=0, tiled=True)  17.1 us
    all_to_all x1, blocking collectives, body(): lax.all_to_all(terms, ('yl', 'x'), split_axis=0, concat_axis=0, tiled=True)  12.1 us
    pallas_call x1, Pallas kernels, attend(): pl.pallas_call(attend_kernel, out_shape=jax.ShapeDtypeStruct((RING, ROWS...  9.36 us
    all_to_all x1, starting transfers between devices, body(): lax.all_to_all(sent, 'z', split_axis=0, concat_axis=0, tiled=True)  8.47 us
    pallas_call x1, Pallas kernels, path_masks(): pl.pallas_call(mask_kernel, out_shape=jax.ShapeDtypeStruct((GROUPS * PAGE...  6.56 us
    all_to_all x1, waiting for transfers between devices, body(): lax.all_to_all(sent, 'z', split_axis=0, concat_axis=0, tiled=True)  6.26 us
    ppermute x6, starting transfers between devices, swap(): return [lax.ppermute(value, axis, [(0, 1), (1, 0)]) for value in values]  4.63 us
    all_to_all x1, starting transfers between devices, body(): parts = lax.all_to_all(parts, 'z', split_axis=0, concat_axis=0, tiled=True)  3.54 us
  transfers between devices with their start and end apart: 8, of which 4 were waited for; matrix products, arithmetic and copies ran while one was open for 4% of the time, Pallas kernels for 10%

profile of v3, /device:TPU:16, one launch (start us, length us, event | category | flops | bytes accessed | tf_op | source)
XLA Modules:
  0.0 80.6 jit_solution(17344283095930455657)
XLA Ops:
  0.0 2.1 %collective-permute-start = (bf16[96,16,128]{2,1,0:T(8,128)(2,1)}, bf16[96,16,128]{2,1,0:T(8,128)(2,1)S(1)}, u32[]{:S(2)}, u32[]{:S(2)}) collective-permute-start(bf16[96,16,128]{2,1,0:T(8,128)(2,1)} %ka_ref.1), channel_id=1, source_target_pairs={{0,128},{128,0},{1,129},{129,1},{2,130},{130,2},{3,131},{131,3},{4... | collective-permute-start | bytes 1179656 | tf_op jit(solution)/shard_map/ppermute | solution.py:296
  2.1 1.5 %collective-permute-start.1 = (bf16[96,16,128]{2,1,0:T(8,128)(2,1)}, bf16[96,16,128]{2,1,0:T(8,128)(2,1)S(1)}, u32[]{:S(2)}, u32[]{:S(2)}) collective-permute-start(bf16[96,16,128]{2,1,0:T(8,128)(2,1)} %va_ref.1), channel_id=1, source_target_pairs={{0,128},{128,0},{1,129},{129,1},{2,130},{130,2},{3,131},{131,3},{4... | collective-permute-start | bytes 1179656 | tf_op jit(solution)/shard_map/ppermute | solution.py:296
  3.5 1.7 %prepare.1.query_ref = bf16[8,32,1152]{2,1,0:T(8,128)(2,1)} custom-call(s32[8]{0:T(128)} %parent_ref.1, bf16[8,4,1024]{2,1,0:T(4,128)(2,1)} %query_ref.1), custom_call_target="tpu_custom_call" | custom-call | flops 1150000000 | bytes 65536 | tf_op jit(solution)/shard_map/prepare/pallas_call | solution.py:42
  5.3 8.5 %all-to-all-start = ((bf16[8,32,1152]{2,1,0:T(8,128)(2,1)}), bf16[8,32,1152]{2,1,0:T(8,128)(2,1)S(1)}, u32[]{:S(2)}, u32[]{:S(2)}) async-start(bf16[8,32,1152]{2,1,0:T(8,128)(2,1)} %prepare.1.query_ref), calls=%async_computation | async-start | bytes 1179648 | tf_op jit(solution)/shard_map/all_to_all | solution.py:293
  13.7 0.0 collective-permute-start.2
  13.7 0.5 collective-permute-start.3
  14.3 1.1 %copy.16 = s32[1024,32]{1,0:T(8,128)S(1)} copy(s32[1024,32]{0,1:T(8,128)} %bitcast.11) | data formatting | bytes 262144 | tf_op jit(solution)/shard_map/transpose | solution.py:309
  15.4 0.2 reshape.48.table_ref
  15.5 0.1 copy.17
  15.6 0.7 sub.30
  16.3 0.1 sub.31
  16.4 0.1 pad_add_fusion.first_ref
  16.5 0.0 copy-start.6
  16.5 0.0 copy-start.2
  16.5 0.0 copy-start.3
  16.5 6.6 %path_masks.1.count_ref = s32[384,128]{1,0:T(8,128)S(1)} custom-call(s32[4]{0:T(128)S(1)} %pad_add_fusion.first_ref, s32[256,128]{1,0:T(8,128)S(1)} %reshape.48.table_ref, s32[256,128]{1,0:T(8,128)S(1)} %subtract_clamp_fusion.left_ref), custom_call_target="tpu_custom_call" | custom-call | flops 8049999872 | bytes 65536 | tf_op jit(solution)/shard_map/path_masks/pallas_call | solution.py:71
  23.1 0.0 copy-done.6
  23.1 0.1 copy.18
  23.2 0.1 reshape.50
  23.3 0.0 collective-permute-done.kc_ref
  23.3 0.0 collective-permute-done.1.vc_ref
  23.3 0.2 collective-permute-start.4
  23.5 0.4 collective-permute-start.5
  23.9 0.1 fusion
  24.0 0.1 and.26
  24.1 0.2 convert_reduce_fusion.1
  24.3 0.2 select_reduce_fusion
  24.5 0.1 reshape.49.list_ref
  24.6 0.1 convert_reduce_fusion.2.used_ref
  24.7 0.0 collective-permute-done.2.kb_ref
  24.7 0.0 collective-permute-done.3.vb_ref
  24.7 0.5 collective-permute-done.4.kd_ref
  25.3 0.6 collective-permute-done.5.vd_ref
  25.8 6.3 %all-to-all-done.query_ref = bf16[8,32,1152]{2,1,0:T(8,128)(2,1)S(1)} async-done(((bf16[8,32,1152]{2,1,0:T(8,128)(2,1)}), bf16[8,32,1152]{2,1,0:T(8,128)(2,1)S(1)}, u32[]{:S(2)}, u32[]{:S(2)}) %all-to-all-start) | async-done | bytes 589856 | tf_op jit(solution)/shard_map/all_to_all | solution.py:293
  32.1 0.0 copy-done.2
  32.1 0.0 copy-done.3
  32.1 9.4 %attend.1 = bf16[8,272,128]{2,1,0:T(8,128)(2,1)} custom-call(s32[384]{0:T(512)S(1)} %reshape.49.list_ref, s32[4]{0:T(128)S(1)} %convert_reduce_fusion.2.used_ref, bf16[8,32,1152]{2,1,0:T(8,128)(2,1)S(1)} %all-to-all-done.query_ref, bf16[96,16,128]{2,1,0:T(8,128)(2,1)S(1)} %copy-done.2, bf16[96,16,128]{2,1,0:T(8,128)(2,1)S(1)} %copy-done.3, ...), custom_call_target="tpu_custom_call" | custom-call | flops 11500000256 | bytes 65536 | tf_op jit(solution)/shard_map/attend/pallas_call | solution.py:189
  41.4 3.5 %all-to-all-start.1 = ((bf16[8,272,128]{2,1,0:T(8,128)(2,1)}), bf16[8,272,128]{2,1,0:T(8,128)(2,1)S(1)}, u32[]{:S(2)}, u32[]{:S(2)}) async-start(bf16[8,272,128]{2,1,0:T(8,128)(2,1)} %attend.1), calls=%async_computation.1 | async-start | bytes 1114112 | tf_op jit(solution)/shard_map/all_to_all | solution.py:326
  45.0 0.0 copy-start
  45.0 0.0 copy-start.4
  45.0 0.0 copy-start.5
  45.0 0.1 permit.1
  45.1 17.1 %all-to-all-done.1.parts_ref = bf16[8,272,128]{2,1,0:T(8,128)(2,1)S(1)} async-done(((bf16[8,272,128]{2,1,0:T(8,128)(2,1)}), bf16[8,272,128]{2,1,0:T(8,128)(2,1)S(1)}, u32[]{:S(2)}, u32[]{:S(2)}) %all-to-all-start.1) | async-done | bytes 557088 | tf_op jit(solution)/shard_map/all_to_all | solution.py:326
  62.2 0.0 copy-done
  62.2 0.0 copy-done.4
  62.2 0.0 copy-done.5
  62.2 0.0 copy-start.1
  62.2 3.4 %copy-done.1 = bf16[1024,4096]{1,0:T(8,128)(2,1)S(1)} copy-done((bf16[1024,4096]{1,0:T(8,128)(2,1)S(1)}, bf16[1024,4096]{1,0:T(8,128)(2,1)}, u32[]{:S(2)}) %copy-start.1) | copy-done | bytes 8388632
  65.6 2.2 %finish.1 = bf16[8,32,512]{2,1,0:T(8,128)(2,1)S(1)} custom-call(bf16[8,272,128]{2,1,0:T(8,128)(2,1)S(1)} %all-to-all-done.1.parts_ref, bf16[8,32,1152]{2,1,0:T(8,128)(2,1)S(1)} %copy-done, bf16[32,128]{1,0:T(8,128)(2,1)S(1)} %bitcast.8, bf16[32,128]{1,0:T(8,128)(2,1)S(1)} %bitcast.9, s32[32,128]{1,0:T(8,128)S(1)} %get-tuple-element.23.allowed_ref, ...), custom_call_target="tpu_custom_call" | custom-call | flops 4600000000 | bytes 65536 | tf_op jit(solution)/shard_map/finish/pallas_call | solution.py:275
  67.8 12.1 %all_to_all.15 = bf16[8,32,512]{2,1,0:T(8,128)(2,1)S(1)} all-to-all(bf16[8,32,512]{2,1,0:T(8,128)(2,1)S(1)} %finish.1), channel_id=1, replica_groups=mesh['yh'=2,'z'=8,'c'=2,'yl'=2,'x'=4] {'yl','x'}, dimensions={0} | all-to-all | bytes 524288 | tf_op jit(solution)/shard_map/all_to_all | solution.py:337
  80.0 0.7 reshape.53
  (6 shorter events, 0.1 us)
Async XLA Ops:
  0.0 23.3 %collective-permute-start = (bf16[96,16,128]{2,1,0:T(8,128)(2,1)}, bf16[96,16,128]{2,1,0:T(8,128)(2,1)S(1)}, u32[]{:S(2)}, u32[]{:S(2)}) collective-permute-start(bf16[96,16,128]{2,1,0:T(8,128)(2,1)} %ka_ref.1), channel_id=1, source_target_pairs={{0,128},{128,0},{1,129},{129,1},{2,130},{130,2},{3,131},{131,3},{4... | collective-permute-start | bytes 1179656 | tf_op jit(solution)/shard_map/ppermute | solution.py:296
  2.1 21.2 %collective-permute-start.1 = (bf16[96,16,128]{2,1,0:T(8,128)(2,1)}, bf16[96,16,128]{2,1,0:T(8,128)(2,1)S(1)}, u32[]{:S(2)}, u32[]{:S(2)}) collective-permute-start(bf16[96,16,128]{2,1,0:T(8,128)(2,1)} %va_ref.1), channel_id=1, source_target_pairs={{0,128},{128,0},{1,129},{129,1},{2,130},{130,2},{3,131},{131,3},{4... | collective-permute-start | bytes 1179656 | tf_op jit(solution)/shard_map/ppermute | solution.py:296
  5.3 26.8 %all-to-all-start = ((bf16[8,32,1152]{2,1,0:T(8,128)(2,1)}), bf16[8,32,1152]{2,1,0:T(8,128)(2,1)S(1)}, u32[]{:S(2)}, u32[]{:S(2)}) async-start(bf16[8,32,1152]{2,1,0:T(8,128)(2,1)} %prepare.1.query_ref), calls=%async_computation | async-start | bytes 1179648 | tf_op jit(solution)/shard_map/all_to_all | solution.py:293
  13.7 11.0 %collective-permute-start.2 = (bf16[96,16,128]{2,1,0:T(8,128)(2,1)}, bf16[96,16,128]{2,1,0:T(8,128)(2,1)S(1)}, u32[]{:S(2)}, u32[]{:S(2)}) collective-permute-start(bf16[96,16,128]{2,1,0:T(8,128)(2,1)} %ka_ref.1), channel_id=1, source_target_pairs={{0,8},{8,0},{1,9},{9,1},{2,10},{10,2},{3,11},{11,3},{4,12},{12,4},... | collective-permute-start | bytes 1179656 | tf_op jit(solution)/shard_map/ppermute | solution.py:296
  13.7 11.0 %collective-permute-start.3 = (bf16[96,16,128]{2,1,0:T(8,128)(2,1)}, bf16[96,16,128]{2,1,0:T(8,128)(2,1)S(1)}, u32[]{:S(2)}, u32[]{:S(2)}) collective-permute-start(bf16[96,16,128]{2,1,0:T(8,128)(2,1)} %va_ref.1), channel_id=1, source_target_pairs={{0,8},{8,0},{1,9},{9,1},{2,10},{10,2},{3,11},{11,3},{4,12},{12,4},... | collective-permute-start | bytes 1179656 | tf_op jit(solution)/shard_map/ppermute | solution.py:296
  16.5 6.6 %copy-start.6 = (s32[8,4]{0,1:T(4,128)S(1)}, s32[8,4]{0,1:T(4,128)}, u32[]{:S(2)}) copy-start(s32[8,4]{0,1:T(4,128)} %param.19) | copy-start | bytes 388
  16.5 15.6 %copy-start.2 = (bf16[96,16,128]{2,1,0:T(8,128)(2,1)S(1)}, bf16[96,16,128]{2,1,0:T(8,128)(2,1)}, u32[]{:S(2)}) copy-start(bf16[96,16,128]{2,1,0:T(8,128)(2,1)} %ka_ref.1) | copy-start | bytes 1179652
  16.5 15.6 %copy-start.3 = (bf16[96,16,128]{2,1,0:T(8,128)(2,1)S(1)}, bf16[96,16,128]{2,1,0:T(8,128)(2,1)}, u32[]{:S(2)}) copy-start(bf16[96,16,128]{2,1,0:T(8,128)(2,1)} %va_ref.1) | copy-start | bytes 1179652
  23.3 1.9 %collective-permute-start.4 = (bf16[96,16,128]{2,1,0:T(8,128)(2,1)S(1)}, bf16[96,16,128]{2,1,0:T(8,128)(2,1)}, u32[]{:S(2)}, u32[]{:S(2)}) collective-permute-start(bf16[96,16,128]{2,1,0:T(8,128)(2,1)S(1)} %collective-permute-done.kc_ref), channel_id=1, source_target_pairs={{0,8},{8,0},{1,9},{9,1},{2,10},{10,2},{3,11},{11,3},{4,12},{12,4},... | collective-permute-start | bytes 1179656 | tf_op jit(solution)/shard_map/ppermute | solution.py:296
  23.5 2.3 %collective-permute-start.5 = (bf16[96,16,128]{2,1,0:T(8,128)(2,1)S(1)}, bf16[96,16,128]{2,1,0:T(8,128)(2,1)}, u32[]{:S(2)}, u32[]{:S(2)}) collective-permute-start(bf16[96,16,128]{2,1,0:T(8,128)(2,1)S(1)} %collective-permute-done.1.vc_ref), channel_id=1, source_target_pairs={{0,8},{8,0},{1,9},{9,1},{2,10},{10,2},{3,11},{11,3},{4,12},{12,4},... | collective-permute-start | bytes 1179656 | tf_op jit(solution)/shard_map/ppermute | solution.py:296
  41.4 20.8 %all-to-all-start.1 = ((bf16[8,272,128]{2,1,0:T(8,128)(2,1)}), bf16[8,272,128]{2,1,0:T(8,128)(2,1)S(1)}, u32[]{:S(2)}, u32[]{:S(2)}) async-start(bf16[8,272,128]{2,1,0:T(8,128)(2,1)} %attend.1), calls=%async_computation.1 | async-start | bytes 1114112 | tf_op jit(solution)/shard_map/all_to_all | solution.py:326
  45.0 17.2 %copy-start = (bf16[8,32,1152]{2,1,0:T(8,128)(2,1)S(1)}, bf16[8,32,1152]{2,1,0:T(8,128)(2,1)}, u32[]{:S(2)}) copy-start(bf16[8,32,1152]{2,1,0:T(8,128)(2,1)} %prepare.1.query_ref) | copy-start | bytes 1769476
  45.0 17.2 %copy-start.4 = (bf16[8,4,128]{2,1,0:T(4,128)(2,1)S(1)}, bf16[8,4,128]{2,1,0:T(4,128)(2,1)}, u32[]{:S(2)}) copy-start(bf16[8,4,128]{2,1,0:T(4,128)(2,1)} %param.11) | copy-start | bytes 24580
  45.0 17.2 %copy-start.5 = (bf16[8,4,128]{2,1,0:T(4,128)(2,1)S(1)}, bf16[8,4,128]{2,1,0:T(4,128)(2,1)}, u32[]{:S(2)}) copy-start(bf16[8,4,128]{2,1,0:T(4,128)(2,1)} %param.12) | copy-start | bytes 24580
  62.2 3.4 %copy-start.1 = (bf16[1024,4096]{1,0:T(8,128)(2,1)S(1)}, bf16[1024,4096]{1,0:T(8,128)(2,1)}, u32[]{:S(2)}) copy-start(bf16[1024,4096]{1,0:T(8,128)(2,1)} %weight_ref.1) | copy-start | bytes 25165828

commit v4 on v3

--- a/solution.py
+++ b/solution.py
@@ -28,23 +28,27 @@
 
 
 def prepare_kernel(parent_ref, query_ref, out_ref, wide):
-    lane = lax.broadcasted_iota(jnp.int32, (4, HD), 1)
-    for child in range(8):
-        rows = slice(child * 4, child * 4 + 4)
-        wide[rows, 0 : HEADS * HD] = query_ref[child].astype(jnp.float32)
-        wide[rows, HEADS * HD : (HEADS + 1) * HD] = jnp.where(lane == parent_ref[child], 1.0, 0.0)
+    child = lax.broadcasted_iota(jnp.int32, (16, HD), 0)
+    lane = lax.broadcasted_iota(jnp.int32, (16, HD), 1)
+    hot = jnp.zeros((16, HD), jnp.float32)
+    for number in range(8):
+        wide[number * 4 : number * 4 + 4, :] = query_ref[number].astype(jnp.float32)
+        hot = jnp.where((child == number) & (lane == parent_ref[number]), 1.0, hot)
+    hot = hot.astype(jnp.bfloat16)
     held = wide[...].astype(jnp.bfloat16)
     for copy in range(RING):
-        out_ref[copy] = held
+        for head in range(HEADS):
+            out_ref[copy, head * CS : (head + 1) * CS, :] = held[:, head * HD : (head + 1) * HD]
+        out_ref[copy, ROWS : ROWS + 16, :] = hot
 
 
 def prepare(parent, queries):
     return pl.pallas_call(
         prepare_kernel,
-        out_shape=jax.ShapeDtypeStruct((RING, CS, (HEADS + 1) * HD), jnp.bfloat16),
+        out_shape=jax.ShapeDtypeStruct((RING, ROWS + 16, HD), jnp.bfloat16),
         in_specs=[pl.BlockSpec(memory_space=pltpu.SMEM), pl.BlockSpec(memory_space=pltpu.VMEM)],
         out_specs=pl.BlockSpec(memory_space=pltpu.VMEM),
-        scratch_shapes=[pltpu.VMEM((CS, (HEADS + 1) * HD), jnp.float32)],
+        scratch_shapes=[pltpu.VMEM((CS, HEADS * HD), jnp.float32)],
         cost_estimate=cost(1.0),
         compiler_params=pltpu.CompilerParams(vmem_limit_bytes=60 * MIB),
         name="prepare",
@@ -143,13 +147,15 @@
 
         lax.fori_loop(0, (used_ref[group] + UNROLL - 1) // UNROLL, some_pages, 0)
         filled = filled + used_ref[group]
-    values[:, HD : 2 * HD] = jnp.ones((values.shape[0], HD), jnp.bfloat16)
+    place = lax.broadcasted_iota(jnp.int32, (CS, 16), 0) // 4
+    spread = jnp.where(lax.broadcasted_iota(jnp.int32, (CS, 16), 1) == place, 1.0, 0.0).astype(jnp.bfloat16)
     for block in range(RING):
-        held = query_ref[block]
+        hot = jnp.dot(spread, query_ref[block, ROWS : ROWS + 16, :], preferred_element_type=jnp.float32)
+        hot = hot.astype(jnp.bfloat16)
+        rows[block * ROWS : (block + 1) * ROWS, 0:HD] = query_ref[block, 0:ROWS, :]
         for head in range(HEADS):
             at = block * ROWS + head * CS
-            rows[at : at + CS, 0:HD] = held[:, head * HD : (head + 1) * HD]
-            rows[at : at + CS, HD : 2 * HD] = held[:, HEADS * HD : (HEADS + 1) * HD]
+            rows[at : at + CS, HD : 2 * HD] = hot
 
     lower = -1
     for tokens in SIZES:
@@ -164,6 +170,7 @@
                 return carry
 
             lax.fori_loop(filled, tokens // PAGE, one_blank, 0)
+            values[0:tokens, HD : 2 * HD] = jnp.ones((tokens, HD), jnp.bfloat16)
             attend_tokens(tokens, rows, keys, values, levels, out_ref)
 
         lower = tokens
@@ -240,7 +247,7 @@
             for half in range(2)
         ]
         levels.append(jnp.concatenate(columns, axis=0))
-    query = jnp.concatenate([query_ref[0, :, head * HD : (head + 1) * HD] for head in range(HEADS)], axis=0)
+    query = query_ref[0, 0:ROWS, :]
     scores = lax.dot_general(
         query, key_ref[...], (((1,), (1,)), ((), ())), preferred_element_type=jnp.float32
     )

time: 81 us -> 80.2 us (level)
  waiting for transfers between devices: 24.5 us -> 23.6 us
where the time goes in v4:
time: 80.2 us; the launch traced here: 79.8 us
  waiting for transfers between devices  23.6 us (29%)
  Pallas kernels  20 us (25%)
  starting transfers between devices  16.6 us (21%)
  blocking collectives  12.1 us (15%)
  local copies, waits for them, and re-layouts  6.51 us (8%)
    all_to_all x1, waiting for transfers between devices, body(): parts = lax.all_to_all(parts, 'z', split_axis=0, concat_axis=0, tiled=True)  17 us
    all_to_all x1, blocking collectives, body(): lax.all_to_all(terms, ('yl', 'x'), split_axis=0, concat_axis=0, tiled=True)  12.1 us
    pallas_call x1, Pallas kernels, attend(): pl.pallas_call(attend_kernel, out_shape=jax.ShapeDtypeStruct((RING, ROWS...  9.4 us
    all_to_all x1, starting transfers between devices, body(): lax.all_to_all(sent, 'z', split_axis=0, concat_axis=0, tiled=True)  8.47 us
    pallas_call x1, Pallas kernels, path_masks(): pl.pallas_call(mask_kernel, out_shape=jax.ShapeDtypeStruct((GROUPS * PAGE...  6.56 us
    all_to_all x1, waiting for transfers between devices, body(): lax.all_to_all(sent, 'z', split_axis=0, concat_axis=0, tiled=True)  5.56 us
    ppermute x6, starting transfers between devices, swap(): return [lax.ppermute(value, axis, [(0, 1), (1, 0)]) for value in values]  4.63 us
    all_to_all x1, starting transfers between devices, body(): parts = lax.all_to_all(parts, 'z', split_axis=0, concat_axis=0, tiled=True)  3.54 us
  transfers between devices with their start and end apart: 8, of which 4 were waited for; matrix products, arithmetic and copies ran while one was open for 4% of the time, Pallas kernels for 10%

profile of v4, /device:TPU:16, one launch (start us, length us, event | category | flops | bytes accessed | tf_op | source)
XLA Modules:
  0.0 79.8 jit_solution(16938449851348787916)
XLA Ops:
  0.0 2.1 %collective-permute-start = (bf16[96,16,128]{2,1,0:T(8,128)(2,1)}, bf16[96,16,128]{2,1,0:T(8,128)(2,1)S(1)}, u32[]{:S(2)}, u32[]{:S(2)}) collective-permute-start(bf16[96,16,128]{2,1,0:T(8,128)(2,1)} %ka_ref.1), channel_id=1, source_target_pairs={{0,128},{128,0},{1,129},{129,1},{2,130},{130,2},{3,131},{131,3},{4... | collective-permute-start | bytes 1179656 | tf_op jit(solution)/shard_map/ppermute | solution.py:303
  2.1 1.5 %collective-permute-start.1 = (bf16[96,16,128]{2,1,0:T(8,128)(2,1)}, bf16[96,16,128]{2,1,0:T(8,128)(2,1)S(1)}, u32[]{:S(2)}, u32[]{:S(2)}) collective-permute-start(bf16[96,16,128]{2,1,0:T(8,128)(2,1)} %va_ref.1), channel_id=1, source_target_pairs={{0,128},{128,0},{1,129},{129,1},{2,130},{130,2},{3,131},{131,3},{4... | collective-permute-start | bytes 1179656 | tf_op jit(solution)/shard_map/ppermute | solution.py:303
  3.5 1.7 %prepare.1.query_ref = bf16[8,272,128]{2,1,0:T(8,128)(2,1)} custom-call(s32[8]{0:T(128)} %parent_ref.1, bf16[8,4,1024]{2,1,0:T(4,128)(2,1)} %query_ref.1), custom_call_target="tpu_custom_call" | custom-call | flops 1150000000 | bytes 65536 | tf_op jit(solution)/shard_map/prepare/pallas_call | solution.py:46
  5.2 8.5 %all-to-all-start = ((bf16[8,272,128]{2,1,0:T(8,128)(2,1)}), bf16[8,272,128]{2,1,0:T(8,128)(2,1)S(1)}, u32[]{:S(2)}, u32[]{:S(2)}) async-start(bf16[8,272,128]{2,1,0:T(8,128)(2,1)} %prepare.1.query_ref), calls=%async_computation | async-start | bytes 1114112 | tf_op jit(solution)/shard_map/all_to_all | solution.py:300
  13.7 0.0 collective-permute-start.2
  13.7 0.5 collective-permute-start.3
  14.2 1.1 %copy.16 = s32[1024,32]{1,0:T(8,128)S(1)} copy(s32[1024,32]{0,1:T(8,128)} %bitcast.11) | data formatting | bytes 262144 | tf_op jit(solution)/shard_map/transpose | solution.py:316
  15.3 0.2 reshape.48.table_ref
  15.5 0.1 copy.17
  15.6 0.7 sub.30
  16.3 0.1 sub.31
  16.4 0.1 pad_add_fusion.first_ref
  16.5 0.0 copy-start.6
  16.5 0.0 copy-start.2
  16.5 0.0 copy-start.3
  16.5 6.6 %path_masks.1.count_ref = s32[384,128]{1,0:T(8,128)S(1)} custom-call(s32[4]{0:T(128)S(1)} %pad_add_fusion.first_ref, s32[256,128]{1,0:T(8,128)S(1)} %reshape.48.table_ref, s32[256,128]{1,0:T(8,128)S(1)} %subtract_clamp_fusion.left_ref), custom_call_target="tpu_custom_call" | custom-call | flops 8049999872 | bytes 65536 | tf_op jit(solution)/shard_map/path_masks/pallas_call | solution.py:75
  23.1 0.0 copy-done.6
  23.1 0.1 copy.18
  23.1 0.1 reshape.50
  23.3 0.0 collective-permute-done.kc_ref
  23.3 0.0 collective-permute-done.1.vc_ref
  23.3 0.2 collective-permute-start.4
  23.5 0.4 collective-permute-start.5
  23.9 0.1 fusion
  24.0 0.1 and.26
  24.1 0.2 convert_reduce_fusion.1
  24.3 0.2 select_reduce_fusion
  24.5 0.1 reshape.49.list_ref
  24.5 0.1 convert_reduce_fusion.2.used_ref
  24.7 0.0 collective-permute-done.2.kb_ref
  24.7 0.0 collective-permute-done.3.vb_ref
  24.7 0.5 collective-permute-done.4.kd_ref
  25.2 0.6 collective-permute-done.5.vd_ref
  25.8 5.6 %all-to-all-done.query_ref = bf16[8,272,128]{2,1,0:T(8,128)(2,1)S(1)} async-done(((bf16[8,272,128]{2,1,0:T(8,128)(2,1)}), bf16[8,272,128]{2,1,0:T(8,128)(2,1)S(1)}, u32[]{:S(2)}, u32[]{:S(2)}) %all-to-all-start) | async-done | bytes 557088 | tf_op jit(solution)/shard_map/all_to_all | solution.py:300
  31.3 0.0 copy-done.2
  31.3 0.0 copy-done.3
  31.3 9.4 %attend.1 = bf16[8,272,128]{2,1,0:T(8,128)(2,1)} custom-call(s32[384]{0:T(512)S(1)} %reshape.49.list_ref, s32[4]{0:T(128)S(1)} %convert_reduce_fusion.2.used_ref, bf16[8,272,128]{2,1,0:T(8,128)(2,1)S(1)} %all-to-all-done.query_ref, bf16[96,16,128]{2,1,0:T(8,128)(2,1)S(1)} %copy-done.2, bf16[96,16,128]{2,1,0:T(8,128)(2,1)S(1)} %copy-done.3, ...), custom_call_target="tpu_custom_call" | custom-call | flops 11500000256 | bytes 65536 | tf_op jit(solution)/shard_map/attend/pallas_call | solution.py:196
  40.7 3.5 %all-to-all-start.1 = ((bf16[8,272,128]{2,1,0:T(8,128)(2,1)}), bf16[8,272,128]{2,1,0:T(8,128)(2,1)S(1)}, u32[]{:S(2)}, u32[]{:S(2)}) async-start(bf16[8,272,128]{2,1,0:T(8,128)(2,1)} %attend.1), calls=%async_computation.1 | async-start | bytes 1114112 | tf_op jit(solution)/shard_map/all_to_all | solution.py:333
  44.3 0.0 copy-start
  44.3 0.0 copy-start.4
  44.3 0.0 copy-start.5
  44.3 0.1 permit.1
  44.4 17.0 %all-to-all-done.1.parts_ref = bf16[8,272,128]{2,1,0:T(8,128)(2,1)S(1)} async-done(((bf16[8,272,128]{2,1,0:T(8,128)(2,1)}), bf16[8,272,128]{2,1,0:T(8,128)(2,1)S(1)}, u32[]{:S(2)}, u32[]{:S(2)}) %all-to-all-start.1) | async-done | bytes 557088 | tf_op jit(solution)/shard_map/all_to_all | solution.py:333
  61.4 0.0 copy-done
  61.4 0.0 copy-done.4
  61.4 0.0 copy-done.5
  61.4 0.0 copy-start.1
  61.4 3.4 %copy-done.1 = bf16[1024,4096]{1,0:T(8,128)(2,1)S(1)} copy-done((bf16[1024,4096]{1,0:T(8,128)(2,1)S(1)}, bf16[1024,4096]{1,0:T(8,128)(2,1)}, u32[]{:S(2)}) %copy-start.1) | copy-done | bytes 8388632
  64.8 2.2 %finish.1 = bf16[8,32,512]{2,1,0:T(8,128)(2,1)S(1)} custom-call(bf16[8,272,128]{2,1,0:T(8,128)(2,1)S(1)} %all-to-all-done.1.parts_ref, bf16[8,272,128]{2,1,0:T(8,128)(2,1)S(1)} %copy-done, bf16[32,128]{1,0:T(8,128)(2,1)S(1)} %bitcast.8, bf16[32,128]{1,0:T(8,128)(2,1)S(1)} %bitcast.9, s32[32,128]{1,0:T(8,128)S(1)} %get-tuple-element.23.allowed_ref, ...), custom_call_target="tpu_custom_call" | custom-call | flops 4600000000 | bytes 65536 | tf_op jit(solution)/shard_map/finish/pallas_call | solution.py:282
  67.0 12.1 %all_to_all.15 = bf16[8,32,512]{2,1,0:T(8,128)(2,1)S(1)} all-to-all(bf16[8,32,512]{2,1,0:T(8,128)(2,1)S(1)} %finish.1), channel_id=1, replica_groups=mesh['yh'=2,'z'=8,'c'=2,'yl'=2,'x'=4] {'yl','x'}, dimensions={0} | all-to-all | bytes 524288 | tf_op jit(solution)/shard_map/all_to_all | solution.py:344
  79.1 0.7 reshape.53
  (6 shorter events, 0.1 us)
Async XLA Ops:
  0.0 23.3 %collective-permute-start = (bf16[96,16,128]{2,1,0:T(8,128)(2,1)}, bf16[96,16,128]{2,1,0:T(8,128)(2,1)S(1)}, u32[]{:S(2)}, u32[]{:S(2)}) collective-permute-start(bf16[96,16,128]{2,1,0:T(8,128)(2,1)} %ka_ref.1), channel_id=1, source_target_pairs={{0,128},{128,0},{1,129},{129,1},{2,130},{130,2},{3,131},{131,3},{4... | collective-permute-start | bytes 1179656 | tf_op jit(solution)/shard_map/ppermute | solution.py:303
  2.1 21.2 %collective-permute-start.1 = (bf16[96,16,128]{2,1,0:T(8,128)(2,1)}, bf16[96,16,128]{2,1,0:T(8,128)(2,1)S(1)}, u32[]{:S(2)}, u32[]{:S(2)}) collective-permute-start(bf16[96,16,128]{2,1,0:T(8,128)(2,1)} %va_ref.1), channel_id=1, source_target_pairs={{0,128},{128,0},{1,129},{129,1},{2,130},{130,2},{3,131},{131,3},{4... | collective-permute-start | bytes 1179656 | tf_op jit(solution)/shard_map/ppermute | solution.py:303
  5.2 26.1 %all-to-all-start = ((bf16[8,272,128]{2,1,0:T(8,128)(2,1)}), bf16[8,272,128]{2,1,0:T(8,128)(2,1)S(1)}, u32[]{:S(2)}, u32[]{:S(2)}) async-start(bf16[8,272,128]{2,1,0:T(8,128)(2,1)} %prepare.1.query_ref), calls=%async_computation | async-start | bytes 1114112 | tf_op jit(solution)/shard_map/all_to_all | solution.py:300
  13.7 11.0 %collective-permute-start.2 = (bf16[96,16,128]{2,1,0:T(8,128)(2,1)}, bf16[96,16,128]{2,1,0:T(8,128)(2,1)S(1)}, u32[]{:S(2)}, u32[]{:S(2)}) collective-permute-start(bf16[96,16,128]{2,1,0:T(8,128)(2,1)} %ka_ref.1), channel_id=1, source_target_pairs={{0,8},{8,0},{1,9},{9,1},{2,10},{10,2},{3,11},{11,3},{4,12},{12,4},... | collective-permute-start | bytes 1179656 | tf_op jit(solution)/shard_map/ppermute | solution.py:303
  13.7 11.0 %collective-permute-start.3 = (bf16[96,16,128]{2,1,0:T(8,128)(2,1)}, bf16[96,16,128]{2,1,0:T(8,128)(2,1)S(1)}, u32[]{:S(2)}, u32[]{:S(2)}) collective-permute-start(bf16[96,16,128]{2,1,0:T(8,128)(2,1)} %va_ref.1), channel_id=1, source_target_pairs={{0,8},{8,0},{1,9},{9,1},{2,10},{10,2},{3,11},{11,3},{4,12},{12,4},... | collective-permute-start | bytes 1179656 | tf_op jit(solution)/shard_map/ppermute | solution.py:303
  16.5 6.6 %copy-start.6 = (s32[8,4]{0,1:T(4,128)S(1)}, s32[8,4]{0,1:T(4,128)}, u32[]{:S(2)}) copy-start(s32[8,4]{0,1:T(4,128)} %param.19) | copy-start | bytes 388
  16.5 14.9 %copy-start.2 = (bf16[96,16,128]{2,1,0:T(8,128)(2,1)S(1)}, bf16[96,16,128]{2,1,0:T(8,128)(2,1)}, u32[]{:S(2)}) copy-start(bf16[96,16,128]{2,1,0:T(8,128)(2,1)} %ka_ref.1) | copy-start | bytes 1179652
  16.5 14.9 %copy-start.3 = (bf16[96,16,128]{2,1,0:T(8,128)(2,1)S(1)}, bf16[96,16,128]{2,1,0:T(8,128)(2,1)}, u32[]{:S(2)}) copy-start(bf16[96,16,128]{2,1,0:T(8,128)(2,1)} %va_ref.1) | copy-start | bytes 1179652
  23.3 1.9 %collective-permute-start.4 = (bf16[96,16,128]{2,1,0:T(8,128)(2,1)S(1)}, bf16[96,16,128]{2,1,0:T(8,128)(2,1)}, u32[]{:S(2)}, u32[]{:S(2)}) collective-permute-start(bf16[96,16,128]{2,1,0:T(8,128)(2,1)S(1)} %collective-permute-done.kc_ref), channel_id=1, source_target_pairs={{0,8},{8,0},{1,9},{9,1},{2,10},{10,2},{3,11},{11,3},{4,12},{12,4},... | collective-permute-start | bytes 1179656 | tf_op jit(solution)/shard_map/ppermute | solution.py:303
  23.5 2.3 %collective-permute-start.5 = (bf16[96,16,128]{2,1,0:T(8,128)(2,1)S(1)}, bf16[96,16,128]{2,1,0:T(8,128)(2,1)}, u32[]{:S(2)}, u32[]{:S(2)}) collective-permute-start(bf16[96,16,128]{2,1,0:T(8,128)(2,1)S(1)} %collective-permute-done.1.vc_ref), channel_id=1, source_target_pairs={{0,8},{8,0},{1,9},{9,1},{2,10},{10,2},{3,11},{11,3},{4,12},{12,4},... | collective-permute-start | bytes 1179656 | tf_op jit(solution)/shard_map/ppermute | solution.py:303
  40.7 20.6 %all-to-all-start.1 = ((bf16[8,272,128]{2,1,0:T(8,128)(2,1)}), bf16[8,272,128]{2,1,0:T(8,128)(2,1)S(1)}, u32[]{:S(2)}, u32[]{:S(2)}) async-start(bf16[8,272,128]{2,1,0:T(8,128)(2,1)} %attend.1), calls=%async_computation.1 | async-start | bytes 1114112 | tf_op jit(solution)/shard_map/all_to_all | solution.py:333
  44.3 17.1 %copy-start = (bf16[8,272,128]{2,1,0:T(8,128)(2,1)S(1)}, bf16[8,272,128]{2,1,0:T(8,128)(2,1)}, u32[]{:S(2)}) copy-start(bf16[8,272,128]{2,1,0:T(8,128)(2,1)} %prepare.1.query_ref) | copy-start | bytes 1671172
  44.3 17.1 %copy-start.4 = (bf16[8,4,128]{2,1,0:T(4,128)(2,1)S(1)}, bf16[8,4,128]{2,1,0:T(4,128)(2,1)}, u32[]{:S(2)}) copy-start(bf16[8,4,128]{2,1,0:T(4,128)(2,1)} %param.11) | copy-start | bytes 24580
  44.3 17.1 %copy-start.5 = (bf16[8,4,128]{2,1,0:T(4,128)(2,1)S(1)}, bf16[8,4,128]{2,1,0:T(4,128)(2,1)}, u32[]{:S(2)}) copy-start(bf16[8,4,128]{2,1,0:T(4,128)(2,1)} %param.12) | copy-start | bytes 24580
  61.4 3.4 %copy-start.1 = (bf16[1024,4096]{1,0:T(8,128)(2,1)S(1)}, bf16[1024,4096]{1,0:T(8,128)(2,1)}, u32[]{:S(2)}) copy-start(bf16[1024,4096]{1,0:T(8,128)(2,1)} %weight_ref.1) | copy-start | bytes 25165828

commit v5 on v4

--- a/solution.py
+++ b/solution.py
@@ -233,10 +233,7 @@
     )(finished)
 
 
-def finish_kernel(
-    parts_ref, query_ref, key_ref, value_ref, allowed_ref, alive_ref, weight_ref, out_ref
-):
-    width = out_ref.shape[2]
+def merge_kernel(parts_ref, query_ref, key_ref, value_ref, allowed_ref, out_ref):
     diagonal = lax.broadcasted_iota(jnp.int32, (HD, HD), 0) == lax.broadcasted_iota(jnp.int32, (HD, HD), 1)
     levels = []
     for block in range(RING):
@@ -267,27 +264,44 @@
         total = total + factor
         summed = summed + factor * parts_ref[block, 0:ROWS, :].astype(jnp.float32)
     result = (summed / total).astype(jnp.bfloat16)
-    attended = jnp.concatenate([result[head * CS : (head + 1) * CS, :] for head in range(HEADS)], axis=1)
-
+    for head in range(HEADS):
+        out_ref[:, head * HD : (head + 1) * HD] = result[head * CS : (head + 1) * CS, :]
+
+
+def merge(parts, query, keys, values, allowed):
+    vmem = pl.BlockSpec(memory_space=pltpu.VMEM)
+    return pl.pallas_call(
+        merge_kernel,
+        out_shape=jax.ShapeDtypeStruct((CS, HEADS * HD), jnp.bfloat16),
+        in_specs=[vmem] * 5,
+        out_specs=vmem,
+        cost_estimate=cost(4.0),
+        compiler_params=pltpu.CompilerParams(vmem_limit_bytes=6 * MIB),
+        name="merge",
+    )(parts, query, keys, values, allowed)
+
+
+def project_kernel(attended_ref, alive_ref, weight_ref, out_ref):
+    width = out_ref.shape[2]
     for part in range(out_ref.shape[0]):
         columns = weight_ref[:, part * width : (part + 1) * width]
-        terms = jnp.dot(attended, columns, preferred_element_type=jnp.float32)
+        terms = jnp.dot(attended_ref[...], columns, preferred_element_type=jnp.float32)
         out_ref[part] = (terms * alive_ref[:, 0:1]).astype(jnp.bfloat16)
 
 
-def finish(parts, query, keys, values, allowed, alive, weight):
+def project(attended, alive, weight):
     blocks = 8
     width = weight.shape[1] // blocks
     vmem = pl.BlockSpec(memory_space=pltpu.VMEM)
     return pl.pallas_call(
-        finish_kernel,
+        project_kernel,
         out_shape=jax.ShapeDtypeStruct((blocks, CS, width), jnp.bfloat16),
-        in_specs=[vmem] * 7,
+        in_specs=[vmem] * 3,
         out_specs=vmem,
-        cost_estimate=cost(4.0),
-        compiler_params=pltpu.CompilerParams(vmem_limit_bytes=12 * MIB),
-        name="finish",
-    )(parts, query, keys, values, allowed, alive, weight)
+        cost_estimate=cost(2.0),
+        compiler_params=pltpu.CompilerParams(vmem_limit_bytes=6 * MIB),
+        name="project",
+    )(attended, alive, weight)
 
 
 def body(
@@ -332,15 +346,8 @@
     allowed, alive = permit(line)
     parts = lax.all_to_all(parts, "z", split_axis=0, concat_axis=0, tiled=True)
 
-    terms = finish(
-        parts,
-        sent,
-        new_keys.reshape(rows, HD),
-        new_values.reshape(rows, HD),
-        allowed,
-        alive,
-        out_weight,
-    )
+    attended = merge(parts, sent, new_keys.reshape(rows, HD), new_values.reshape(rows, HD), allowed)
+    terms = project(attended, alive, out_weight)
     terms = lax.all_to_all(terms, ("yl", "x"), split_axis=0, concat_axis=0, tiled=True)
     return jnp.sum(terms.astype(jnp.float32), axis=0).reshape(children, steps, terms.shape[-1])
 

time: 80.2 us -> 80.4 us (level)
    pallas_call x1 -> x2, Pallas kernels: 2.21 us -> 2.43 us  [the longest x1 1.55 us: project(): pl.pallas_call(project_kernel, out_shape=jax.ShapeDtypeStruct((blocks, CS...]
where the time goes in v5:
time: 80.4 us; the launch traced here: 80 us
  waiting for transfers between devices  23.6 us (29%)
  Pallas kernels  20.1 us (25%)
  starting transfers between devices  16.6 us (21%)
  blocking collectives  12.1 us (15%)
  local copies, waits for them, and re-layouts  6.51 us (8%)
    all_to_all x1, waiting for transfers between devices, body(): parts = lax.all_to_all(parts, 'z', split_axis=0, concat_axis=0, tiled=True)  17 us
    all_to_all x1, blocking collectives, body(): lax.all_to_all(terms, ('yl', 'x'), split_axis=0, concat_axis=0, tiled=True)  12.1 us
    pallas_call x1, Pallas kernels, attend(): pl.pallas_call(attend_kernel, out_shape=jax.ShapeDtypeStruct((RING, ROWS...  9.35 us
    all_to_all x1, starting transfers between devices, body(): lax.all_to_all(sent, 'z', split_axis=0, concat_axis=0, tiled=True)  8.47 us
    pallas_call x1, Pallas kernels, path_masks(): pl.pallas_call(mask_kernel, out_shape=jax.ShapeDtypeStruct((GROUPS * PAGE...  6.56 us
    all_to_all x1, waiting for transfers between devices, body(): lax.all_to_all(sent, 'z', split_axis=0, concat_axis=0, tiled=True)  5.56 us
    ppermute x6, starting transfers between devices, swap(): return [lax.ppermute(value, axis, [(0, 1), (1, 0)]) for value in values]  4.63 us
    all_to_all x1, starting transfers between devices, body(): parts = lax.all_to_all(parts, 'z', split_axis=0, concat_axis=0, tiled=True)  3.54 us
  transfers between devices with their start and end apart: 8, of which 4 were waited for; matrix products, arithmetic and copies ran while one was open for 4% of the time, Pallas kernels for 10%

profile of v5, /device:TPU:16, one launch (start us, length us, event | category | flops | bytes accessed | tf_op | source)
XLA Modules:
  0.0 80.0 jit_solution(14585257030974921715)
XLA Ops:
  0.0 2.1 %collective-permute-start = (bf16[96,16,128]{2,1,0:T(8,128)(2,1)}, bf16[96,16,128]{2,1,0:T(8,128)(2,1)S(1)}, u32[]{:S(2)}, u32[]{:S(2)}) collective-permute-start(bf16[96,16,128]{2,1,0:T(8,128)(2,1)} %ka_ref.1), channel_id=1, source_target_pairs={{0,128},{128,0},{1,129},{129,1},{2,130},{130,2},{3,131},{131,3},{4... | collective-permute-start | bytes 1179656 | tf_op jit(solution)/shard_map/ppermute | solution.py:317
  2.1 1.5 %collective-permute-start.1 = (bf16[96,16,128]{2,1,0:T(8,128)(2,1)}, bf16[96,16,128]{2,1,0:T(8,128)(2,1)S(1)}, u32[]{:S(2)}, u32[]{:S(2)}) collective-permute-start(bf16[96,16,128]{2,1,0:T(8,128)(2,1)} %va_ref.1), channel_id=1, source_target_pairs={{0,128},{128,0},{1,129},{129,1},{2,130},{130,2},{3,131},{131,3},{4... | collective-permute-start | bytes 1179656 | tf_op jit(solution)/shard_map/ppermute | solution.py:317
  3.5 1.7 %prepare.1.query_ref = bf16[8,272,128]{2,1,0:T(8,128)(2,1)} custom-call(s32[8]{0:T(128)} %parent_ref.1, bf16[8,4,1024]{2,1,0:T(4,128)(2,1)} %query_ref.1), custom_call_target="tpu_custom_call" | custom-call | flops 1150000000 | bytes 65536 | tf_op jit(solution)/shard_map/prepare/pallas_call | solution.py:46
  5.2 8.5 %all-to-all-start = ((bf16[8,272,128]{2,1,0:T(8,128)(2,1)}), bf16[8,272,128]{2,1,0:T(8,128)(2,1)S(1)}, u32[]{:S(2)}, u32[]{:S(2)}) async-start(bf16[8,272,128]{2,1,0:T(8,128)(2,1)} %prepare.1.query_ref), calls=%async_computation | async-start | bytes 1114112 | tf_op jit(solution)/shard_map/all_to_all | solution.py:314
  13.7 0.0 collective-permute-start.2
  13.7 0.5 collective-permute-start.3
  14.2 1.1 %copy.16 = s32[1024,32]{1,0:T(8,128)S(1)} copy(s32[1024,32]{0,1:T(8,128)} %bitcast.11) | data formatting | bytes 262144 | tf_op jit(solution)/shard_map/transpose | solution.py:330
  15.3 0.2 reshape.48.table_ref
  15.5 0.1 copy.17
  15.6 0.7 sub.30
  16.3 0.1 sub.31
  16.4 0.1 pad_add_fusion.first_ref
  16.5 0.0 copy-start.6
  16.5 0.0 copy-start.2
  16.5 0.0 copy-start.3
  16.5 6.6 %path_masks.1.count_ref = s32[384,128]{1,0:T(8,128)S(1)} custom-call(s32[4]{0:T(128)S(1)} %pad_add_fusion.first_ref, s32[256,128]{1,0:T(8,128)S(1)} %reshape.48.table_ref, s32[256,128]{1,0:T(8,128)S(1)} %subtract_clamp_fusion.left_ref), custom_call_target="tpu_custom_call" | custom-call | flops 8049999872 | bytes 65536 | tf_op jit(solution)/shard_map/path_masks/pallas_call | solution.py:75
  23.1 0.0 copy-done.6
  23.1 0.1 copy.18
  23.1 0.1 reshape.50
  23.3 0.0 collective-permute-done.kc_ref
  23.3 0.0 collective-permute-done.1.vc_ref
  23.3 0.2 collective-permute-start.4
  23.5 0.4 collective-permute-start.5
  23.9 0.1 fusion
  24.0 0.1 and.26
  24.1 0.2 convert_reduce_fusion.1
  24.3 0.2 select_reduce_fusion
  24.5 0.1 reshape.49.list_ref
  24.5 0.1 convert_reduce_fusion.2.used_ref
  24.7 0.0 collective-permute-done.2.kb_ref
  24.7 0.0 collective-permute-done.3.vb_ref
  24.7 0.5 collective-permute-done.4.kd_ref
  25.2 0.6 collective-permute-done.5.vd_ref
  25.8 5.6 %all-to-all-done.query_ref = bf16[8,272,128]{2,1,0:T(8,128)(2,1)S(1)} async-done(((bf16[8,272,128]{2,1,0:T(8,128)(2,1)}), bf16[8,272,128]{2,1,0:T(8,128)(2,1)S(1)}, u32[]{:S(2)}, u32[]{:S(2)}) %all-to-all-start) | async-done | bytes 557088 | tf_op jit(solution)/shard_map/all_to_all | solution.py:314
  31.3 0.0 copy-done.2
  31.3 0.0 copy-done.3
  31.3 9.3 %attend.1 = bf16[8,272,128]{2,1,0:T(8,128)(2,1)} custom-call(s32[384]{0:T(512)S(1)} %reshape.49.list_ref, s32[4]{0:T(128)S(1)} %convert_reduce_fusion.2.used_ref, bf16[8,272,128]{2,1,0:T(8,128)(2,1)S(1)} %all-to-all-done.query_ref, bf16[96,16,128]{2,1,0:T(8,128)(2,1)S(1)} %copy-done.2, bf16[96,16,128]{2,1,0:T(8,128)(2,1)S(1)} %copy-done.3, ...), custom_call_target="tpu_custom_call" | custom-call | flops 11500000256 | bytes 65536 | tf_op jit(solution)/shard_map/attend/pallas_call | solution.py:196
  40.7 3.5 %all-to-all-start.1 = ((bf16[8,272,128]{2,1,0:T(8,128)(2,1)}), bf16[8,272,128]{2,1,0:T(8,128)(2,1)S(1)}, u32[]{:S(2)}, u32[]{:S(2)}) async-start(bf16[8,272,128]{2,1,0:T(8,128)(2,1)} %attend.1), calls=%async_computation.1 | async-start | bytes 1114112 | tf_op jit(solution)/shard_map/all_to_all | solution.py:347
  44.2 0.0 copy-start.1
  44.2 0.0 copy-start.4
  44.3 0.0 copy-start.5
  44.3 0.1 permit.1
  44.4 17.0 %all-to-all-done.1.parts_ref = bf16[8,272,128]{2,1,0:T(8,128)(2,1)S(1)} async-done(((bf16[8,272,128]{2,1,0:T(8,128)(2,1)}), bf16[8,272,128]{2,1,0:T(8,128)(2,1)S(1)}, u32[]{:S(2)}, u32[]{:S(2)}) %all-to-all-start.1) | async-done | bytes 557088 | tf_op jit(solution)/shard_map/all_to_all | solution.py:347
  61.3 0.0 copy-done.1
  61.3 0.0 copy-done.4
  61.3 0.0 copy-done.5
  61.4 0.9 %merge.1.attended_ref = bf16[32,1024]{1,0:T(8,128)(2,1)S(1)} custom-call(bf16[8,272,128]{2,1,0:T(8,128)(2,1)S(1)} %all-to-all-done.1.parts_ref, bf16[8,272,128]{2,1,0:T(8,128)(2,1)S(1)} %copy-done.1, bf16[32,128]{1,0:T(8,128)(2,1)S(1)} %bitcast.8, bf16[32,128]{1,0:T(8,128)(2,1)S(1)} %bitcast.9, s32[32,128]{1,0:T(8,128)S(1)} %get-tuple-element.23.allowed_ref), custom_call_target="tpu_custom_call" | custom-call | flops 4600000000 | bytes 65536 | tf_op jit(solution)/shard_map/merge/pallas_call | solution.py:273
  62.2 0.0 copy-start
  62.2 3.4 %copy-done = bf16[1024,4096]{1,0:T(8,128)(2,1)S(1)} copy-done((bf16[1024,4096]{1,0:T(8,128)(2,1)S(1)}, bf16[1024,4096]{1,0:T(8,128)(2,1)}, u32[]{:S(2)}) %copy-start) | copy-done | bytes 8388632
  65.6 1.6 %project.1 = bf16[8,32,512]{2,1,0:T(8,128)(2,1)S(1)} custom-call(bf16[32,1024]{1,0:T(8,128)(2,1)S(1)} %merge.1.attended_ref, f32[32,128]{1,0:T(8,128)S(1)} %get-tuple-element.24.alive_ref, bf16[1024,4096]{1,0:T(8,128)(2,1)S(1)} %copy-done), custom_call_target="tpu_custom_call" | custom-call | flops 2300000000 | bytes 65536 | tf_op jit(solution)/shard_map/project/pallas_call | solution.py:296
  67.2 12.1 %all_to_all.15 = bf16[8,32,512]{2,1,0:T(8,128)(2,1)S(1)} all-to-all(bf16[8,32,512]{2,1,0:T(8,128)(2,1)S(1)} %project.1), channel_id=1, replica_groups=mesh['yh'=2,'z'=8,'c'=2,'yl'=2,'x'=4] {'yl','x'}, dimensions={0} | all-to-all | bytes 524288 | tf_op jit(solution)/shard_map/all_to_all | solution.py:351
  79.3 0.7 reshape.53
  (6 shorter events, 0.1 us)
Async XLA Ops:
  0.0 23.3 %collective-permute-start = (bf16[96,16,128]{2,1,0:T(8,128)(2,1)}, bf16[96,16,128]{2,1,0:T(8,128)(2,1)S(1)}, u32[]{:S(2)}, u32[]{:S(2)}) collective-permute-start(bf16[96,16,128]{2,1,0:T(8,128)(2,1)} %ka_ref.1), channel_id=1, source_target_pairs={{0,128},{128,0},{1,129},{129,1},{2,130},{130,2},{3,131},{131,3},{4... | collective-permute-start | bytes 1179656 | tf_op jit(solution)/shard_map/ppermute | solution.py:317
  2.1 21.2 %collective-permute-start.1 = (bf16[96,16,128]{2,1,0:T(8,128)(2,1)}, bf16[96,16,128]{2,1,0:T(8,128)(2,1)S(1)}, u32[]{:S(2)}, u32[]{:S(2)}) collective-permute-start(bf16[96,16,128]{2,1,0:T(8,128)(2,1)} %va_ref.1), channel_id=1, source_target_pairs={{0,128},{128,0},{1,129},{129,1},{2,130},{130,2},{3,131},{131,3},{4... | collective-permute-start | bytes 1179656 | tf_op jit(solution)/shard_map/ppermute | solution.py:317
  5.2 26.1 %all-to-all-start = ((bf16[8,272,128]{2,1,0:T(8,128)(2,1)}), bf16[8,272,128]{2,1,0:T(8,128)(2,1)S(1)}, u32[]{:S(2)}, u32[]{:S(2)}) async-start(bf16[8,272,128]{2,1,0:T(8,128)(2,1)} %prepare.1.query_ref), calls=%async_computation | async-start | bytes 1114112 | tf_op jit(solution)/shard_map/all_to_all | solution.py:314
  13.7 11.0 %collective-permute-start.2 = (bf16[96,16,128]{2,1,0:T(8,128)(2,1)}, bf16[96,16,128]{2,1,0:T(8,128)(2,1)S(1)}, u32[]{:S(2)}, u32[]{:S(2)}) collective-permute-start(bf16[96,16,128]{2,1,0:T(8,128)(2,1)} %ka_ref.1), channel_id=1, source_target_pairs={{0,8},{8,0},{1,9},{9,1},{2,10},{10,2},{3,11},{11,3},{4,12},{12,4},... | collective-permute-start | bytes 1179656 | tf_op jit(solution)/shard_map/ppermute | solution.py:317
  13.7 11.0 %collective-permute-start.3 = (bf16[96,16,128]{2,1,0:T(8,128)(2,1)}, bf16[96,16,128]{2,1,0:T(8,128)(2,1)S(1)}, u32[]{:S(2)}, u32[]{:S(2)}) collective-permute-start(bf16[96,16,128]{2,1,0:T(8,128)(2,1)} %va_ref.1), channel_id=1, source_target_pairs={{0,8},{8,0},{1,9},{9,1},{2,10},{10,2},{3,11},{11,3},{4,12},{12,4},... | collective-permute-start | bytes 1179656 | tf_op jit(solution)/shard_map/ppermute | solution.py:317
  16.5 6.6 %copy-start.6 = (s32[8,4]{0,1:T(4,128)S(1)}, s32[8,4]{0,1:T(4,128)}, u32[]{:S(2)}) copy-start(s32[8,4]{0,1:T(4,128)} %param.19) | copy-start | bytes 388
  16.5 14.9 %copy-start.2 = (bf16[96,16,128]{2,1,0:T(8,128)(2,1)S(1)}, bf16[96,16,128]{2,1,0:T(8,128)(2,1)}, u32[]{:S(2)}) copy-start(bf16[96,16,128]{2,1,0:T(8,128)(2,1)} %ka_ref.1) | copy-start | bytes 1179652
  16.5 14.9 %copy-start.3 = (bf16[96,16,128]{2,1,0:T(8,128)(2,1)S(1)}, bf16[96,16,128]{2,1,0:T(8,128)(2,1)}, u32[]{:S(2)}) copy-start(bf16[96,16,128]{2,1,0:T(8,128)(2,1)} %va_ref.1) | copy-start | bytes 1179652
  23.3 1.9 %collective-permute-start.4 = (bf16[96,16,128]{2,1,0:T(8,128)(2,1)S(1)}, bf16[96,16,128]{2,1,0:T(8,128)(2,1)}, u32[]{:S(2)}, u32[]{:S(2)}) collective-permute-start(bf16[96,16,128]{2,1,0:T(8,128)(2,1)S(1)} %collective-permute-done.kc_ref), channel_id=1, source_target_pairs={{0,8},{8,0},{1,9},{9,1},{2,10},{10,2},{3,11},{11,3},{4,12},{12,4},... | collective-permute-start | bytes 1179656 | tf_op jit(solution)/shard_map/ppermute | solution.py:317
  23.5 2.3 %collective-permute-start.5 = (bf16[96,16,128]{2,1,0:T(8,128)(2,1)S(1)}, bf16[96,16,128]{2,1,0:T(8,128)(2,1)}, u32[]{:S(2)}, u32[]{:S(2)}) collective-permute-start(bf16[96,16,128]{2,1,0:T(8,128)(2,1)S(1)} %collective-permute-done.1.vc_ref), channel_id=1, source_target_pairs={{0,8},{8,0},{1,9},{9,1},{2,10},{10,2},{3,11},{11,3},{4,12},{12,4},... | collective-permute-start | bytes 1179656 | tf_op jit(solution)/shard_map/ppermute | solution.py:317
  40.7 20.6 %all-to-all-start.1 = ((bf16[8,272,128]{2,1,0:T(8,128)(2,1)}), bf16[8,272,128]{2,1,0:T(8,128)(2,1)S(1)}, u32[]{:S(2)}, u32[]{:S(2)}) async-start(bf16[8,272,128]{2,1,0:T(8,128)(2,1)} %attend.1), calls=%async_computation.1 | async-start | bytes 1114112 | tf_op jit(solution)/shard_map/all_to_all | solution.py:347
  44.2 17.1 %copy-start.1 = (bf16[8,272,128]{2,1,0:T(8,128)(2,1)S(1)}, bf16[8,272,128]{2,1,0:T(8,128)(2,1)}, u32[]{:S(2)}) copy-start(bf16[8,272,128]{2,1,0:T(8,128)(2,1)} %prepare.1.query_ref) | copy-start | bytes 1671172
  44.2 17.1 %copy-start.4 = (bf16[8,4,128]{2,1,0:T(4,128)(2,1)S(1)}, bf16[8,4,128]{2,1,0:T(4,128)(2,1)}, u32[]{:S(2)}) copy-start(bf16[8,4,128]{2,1,0:T(4,128)(2,1)} %param.11) | copy-start | bytes 24580
  44.3 17.1 %copy-start.5 = (bf16[8,4,128]{2,1,0:T(4,128)(2,1)S(1)}, bf16[8,4,128]{2,1,0:T(4,128)(2,1)}, u32[]{:S(2)}) copy-start(bf16[8,4,128]{2,1,0:T(4,128)(2,1)} %param.12) | copy-start | bytes 24580
  62.2 3.4 %copy-start = (bf16[1024,4096]{1,0:T(8,128)(2,1)S(1)}, bf16[1024,4096]{1,0:T(8,128)(2,1)}, u32[]{:S(2)}) copy-start(bf16[1024,4096]{1,0:T(8,128)(2,1)} %weight_ref.1) | copy-start | bytes 25165828
